TPU v7x, 128 devices: a whole 4x4x4 slice. The times are simulated.
128 devices in a mesh: item: 16 (over z, y), code: 8 (over x, core).
Axes of the slice: x: 4, y: 4, z: 4, core: 2. Of those that a mesh axis runs over, the one named last changes fastest.
Arguments:
- residuals: float32 [256, 65536], P('code', 'item'), may hold values from -6 to 6
- codebook: float32 [256, 65536], P('item', 'code'), may hold values from -6 to 6
- item_weight: float32 [65536], P('item'), may hold values from 1 to 100
- code_capacity: float32 [65536], P('code'), may hold values from 0.25 to 4
- pairs: int32 [1024, 128], P('item', 'code'), may hold values from -1 to 127, as said below
Outputs:
- item_potential: float32 [65536], P('item')
- code_potential: float32 [65536], P('code')
Inputs may be any that keep to these rules, and one draw needn't show every extreme that they name: `pairs`: each entry is -1 (no candidate) or a code block's number within the code shard of its slot column. Within one item block and one code shard the live entries are distinct, the first slot is always live, and between 1 and 8 are live; some device holds exactly 8 live slots in every item block. Every code block is named by some item block.
All inputs are finite; a program needn't handle non-finite values.
Results may differ from a plain program's by a relative error of at most 0.0003.
Values sent between devices are 32-bit elements; how exact they have to be, the bound alone decides.
A program may use at most 128 MiB of HBM per device.

v0:
```python
import math

import jax
import jax.numpy as jnp
from jax import lax
from jax.sharding import PartitionSpec as P

BLOCK = 64
ITERS = 3


masked_score = -1e30
softness_factor = 0.1


def body(residuals, codebook, item_weight, code_capacity, pairs):
    item_columns = lax.all_gather(residuals, "code", axis=0, tiled=True)
    code_cols = lax.all_gather(codebook, "item", axis=0, tiled=True)
    embedding_width = item_columns.shape[0]
    item_count = item_columns.shape[1]
    code_count = code_cols.shape[1]
    item_blocks = item_count // BLOCK
    code_blocks = code_count // BLOCK
    logit_scale = 1.0 / (softness_factor * math.sqrt(embedding_width))
    weight_sum = lax.psum(jnp.sum(item_weight), "item")
    capacity_sum = lax.psum(jnp.sum(code_capacity), "code")
    item_logmass = jnp.log(item_weight) - jnp.log(weight_sum)
    code_logmass = jnp.log(code_capacity) - jnp.log(capacity_sum)
    is_live = pairs >= 0
    safe_ids = jnp.where(is_live, pairs, 0)
    target = jnp.where(is_live, pairs, code_blocks)
    item_split_cols = item_columns.reshape(embedding_width, item_blocks, BLOCK)
    code_column_splits = code_cols.reshape(embedding_width, code_blocks, BLOCK)
    group = math.gcd(item_blocks, 8)
    group_count = item_blocks // group

    def build_tiles(own, ids, live):
        picked = code_column_splits[:, ids, :]
        scores = (
            jnp.einsum("rbi,rbsj->bsij", own, picked, precision=lax.Precision.HIGHEST) * logit_scale
        )
        return jnp.where(live[:, :, None, None], scores, masked_score)

    reduce_fn = lambda tiles, ids, portion: tiles

    def one_group(group_index):
        start = group_index * group
        own = lax.dynamic_slice_in_dim(item_split_cols, start, group, 1)
        ids = lax.dynamic_slice_in_dim(safe_ids, start, group, 0)
        live = lax.dynamic_slice_in_dim(is_live, start, group, 0)
        portion = lax.dynamic_slice_in_dim(safe_ids, start, group, 0)
        return reduce_fn(build_tiles(own, ids, live), ids, portion)

    results = lax.map(one_group, jnp.arange(group_count, dtype=jnp.int32))
    saved_tile_blocks = results.reshape((item_blocks,) + results.shape[2:])

    def run_pass(reduce_fn, extra):
        return reduce_fn(saved_tile_blocks, safe_ids, extra)

    flat_target = target.reshape(-1)
    flat_rows = flat_target.shape[0]
    row_group = math.gcd(flat_rows, 256)
    one_hot = flat_target[:, None] == jnp.arange(code_blocks, dtype=jnp.int32)[None, :]
    one_hot_groups = one_hot.reshape(flat_rows // row_group, row_group, code_blocks)
    one_hot_float = one_hot.astype(jnp.float32)
    code_potential = jnp.zeros((code_count,), jnp.float32)
    item_potential = jnp.zeros((item_count,), jnp.float32)
    for sweep in range(ITERS):
        code_split = code_potential.reshape(code_blocks, BLOCK)

        def row_reduce(tiles, ids, portion):
            logits = tiles + code_split[ids][:, :, None, :]
            block_peak = jnp.max(logits, axis=(1, 3))
            block_total = jnp.sum(jnp.exp(logits - block_peak[:, None, :, None]), axis=(1, 3))
            return (block_peak, block_total)

        row_peak, row_total = run_pass(row_reduce, safe_ids)
        row_peak = row_peak.reshape(item_count)
        row_total = row_total.reshape(item_count)
        merged_peak = lax.pmax(row_peak, "code")
        merged_total = lax.psum(row_total * jnp.exp(row_peak - merged_peak), "code")
        item_potential = item_logmass - (merged_peak + jnp.log(merged_total))
        item_split = item_potential.reshape(item_blocks, BLOCK)

        def col_reduce(tiles, ids, portion):
            logits = tiles + portion[:, None, :, None]
            block_peak = jnp.max(logits, axis=2)
            block_total = jnp.sum(jnp.exp(logits - block_peak[:, :, None, :]), axis=2)
            return (block_peak, block_total)

        tile_peak, tile_total = run_pass(col_reduce, item_split)
        peak_flat = tile_peak.reshape(flat_rows, BLOCK)
        total_flat = tile_total.reshape(flat_rows, BLOCK)
        peak_groups = peak_flat.reshape(flat_rows // row_group, row_group, BLOCK)

        def peak_step(carry, pieces):
            hot, peaks = pieces
            candidate = jnp.max(jnp.where(hot[:, :, None], peaks[:, None, :], masked_score), axis=0)
            return (jnp.maximum(carry, candidate), None)

        col_peak, unused = lax.scan(
            peak_step,
            jnp.full((code_blocks, BLOCK), masked_score, jnp.float32),
            (one_hot_groups, peak_groups),
        )
        padded_peak = jnp.concatenate(
            [col_peak, jnp.full((1, BLOCK), masked_score, jnp.float32)], axis=0
        )
        spread = total_flat * jnp.exp(peak_flat - padded_peak[flat_target])
        col_total = jnp.dot(
            one_hot_float.T,
            spread,
            precision=lax.Precision.HIGHEST,
            preferred_element_type=jnp.float32,
        )
        col_peak = col_peak.reshape(code_count)
        col_total = col_total.reshape(code_count)
        joined_peak = lax.pmax(col_peak, "item")
        joined_total = lax.psum(col_total * jnp.exp(col_peak - joined_peak), "item")
        code_potential = code_logmass - (joined_peak + jnp.log(joined_total))
    return (item_potential, code_potential)


def solution(mesh):
    placed = (P("code", "item"), P("item", "code"), P("item"), P("code"), P("item", "code"))
    return jax.shard_map(
        body, mesh=mesh, in_specs=placed, out_specs=(P("item"), P("code")), check_vma=False
    )
```

profile of v0, /device:TPU:0, one launch (start us, length us, event | category | flops | bytes accessed | tf_op | source)
XLA Modules:
  0.0 1095.5 jit_solution(9727637983515556993)
XLA Ops:
  10.0 42.6 %psum.56 = f32[]{:T(128)} all-reduce(f32[]{:T(128)} %reduce_sum.72), channel_id=1, replica_groups=mesh['item'=16,'code'=8] {'item'}, use_global_device_ids=true, to_apply=%region_1.0 | all-reduce | flops 1 | bytes 8 | tf_op jit(solution)/shard_map/psum | solution.py:25
  64.6 52.7 %all-gather.3.cloned.1.call-done = f32[256,8192]{1,0:T(8,128)} async-done(((f32[16,8192]{1,0:T(8,128)}), f32[256,8192]{1,0:T(8,128)}) %all-gather.3.cloned.1.call-update) | async-done | bytes 8388624 | tf_op jit(solution)/shard_map/all_gather | solution.py:18
  126.3 158.7 %while.43 = (s32[]{:T(128)}, f32[8,8,16,64,64]{3,4,2,1,0:T(8,128)}, s32[8]{0:T(128)S(1)}, pred[64,16]{1,0:T(8,128)(4,1)S(1)}, s32[64,16]{1,0:T(8,128)S(1)}, /*in...) while((s32[]{:T(128)}, f32[8,8,16,64,64]{3,4,2,1,0:T(8,128)}, ...), condition=%wide.region_3.0_spmd, body=%wide.region_2.0_spmd.sunk | while | flops 1611662720 | bytes 29892660 | solution.py:54
  308.9 25.5 %pmax.42 = f32[4096]{0:T(1024)S(1)} all-reduce(f32[4096]{0:T(1024)S(1)} %reshape.211), channel_id=1, replica_groups=mesh['item'=16,'code'=8] {'code'}, use_global_device_ids=true, to_apply=%region_7.8 | all-reduce | flops 4096 | bytes 32768 | tf_op jit(solution)/shard_map/pmax | solution.py:80
  334.4 24.6 %all-reduce.3 = (f32[4096]{0:T(1024)S(1)}, f32[]{:T(128)}) all-reduce(f32[4096]{0:T(1024)S(1)} %exponential_multiply_fusion.5, f32[]{:T(128)} %reduce_sum.73), channel_id=1, replica_groups=mesh['item'=16,'code'=8] {'code'}, use_global_device_ids=true, to_apply=%region_9.10 | all-reduce | flops 4097 | bytes 32776 | tf_op jit(solution)/shard_map/psum | solution.py:81
  359.1 15.3 %add_reduce_fusion.4 = f32[8,8,16,64]{3,2,1,0:T(8,128)S(1)} fusion(f32[8,8,16,64,64]{3,4,2,1,0:T(8,128)} %get-tuple-element.105, f32[8,8,64]{2,1,0:T(8,128)S(1)} %add.154), kind=kLoop, calls=%fused_computation.36 | loop fusion | flops 8323072 | bytes 17055744 | tf_op jit(solution)/shard_map/reduce_max | solution.py:87
  374.4 20.7 %exponential_reduce_fusion.4 = f32[8,8,16,64]{3,2,1,0:T(8,128)S(1)} fusion(f32[8,8,16,64,64]{3,4,2,1,0:T(8,128)} %get-tuple-element.105, f32[8,8,16,64]{3,2,1,0:T(8,128)S(1)} %add_reduce_fusion.4, f32[8,8,64]{2,1,0:T(8,128)S(1)} %add.154), kind=kLoop, calls=%fused_computation.30 | loop fusion | flops 12517376 | bytes 17317888 | tf_op jit(solution)/shard_map/reduce_sum | solution.py:88
  395.1 13.3 %while.44 = (s32[]{:T(128)}, f32[128,64]{0,1:T(8,128)S(1)}, pred[4,256,128]{2,1,0:T(8,128)(4,1)S(1)}, f32[4,256,64]{2,1,0:T(8,128)S(1)}, s32[]{:T(128)}, /*index=5*/s32[]{:T(128)}) while((s32[]{:T(128)}, f32[128,64]{0,1:T(8,128)S(1)}, pred[4,256,128]{2,1,0:T(8,128)(4,1)S(1)}, f32[4,256,64]{2,1,0:T(8,128)S(1)}, s32[]{:T(128)}, ...), condition=%wide.region_13.14_spmd.clone, body=%wide.region_11.13_spmd.clone.sunk | while | flops 4202499 | bytes 426071 | solution.py:101
  412.4 72.4 %pmax.43 = f32[8192]{0:T(1024)S(1)} all-reduce(f32[8192]{0:T(1024)S(1)} %reshape.213), channel_id=1, replica_groups=mesh['item'=16,'code'=8] {'item'}, use_global_device_ids=true, to_apply=%region_14.15 | all-reduce | flops 8192 | bytes 65536 | tf_op jit(solution)/shard_map/pmax | solution.py:118
  484.8 69.5 %psum.59 = f32[8192]{0:T(1024)S(1)} all-reduce(f32[8192]{0:T(1024)S(1)} %exponential_multiply_fusion.2), channel_id=1, replica_groups=mesh['item'=16,'code'=8] {'item'}, use_global_device_ids=true, to_apply=%region_16.17 | all-reduce | flops 8192 | bytes 65536 | tf_op jit(solution)/shard_map/psum | solution.py:119
  581.9 23.5 %pmax.44 = f32[4096]{0:T(1024)S(1)} all-reduce(f32[4096]{0:T(1024)S(1)} %reshape.219), channel_id=1, replica_groups=mesh['item'=16,'code'=8] {'code'}, use_global_device_ids=true, to_apply=%region_18.19 | all-reduce | flops 4096 | bytes 32768 | tf_op jit(solution)/shard_map/pmax | solution.py:80
  605.4 23.6 %psum.60 = f32[4096]{0:T(1024)S(1)} all-reduce(f32[4096]{0:T(1024)S(1)} %exponential_multiply_fusion.4), channel_id=1, replica_groups=mesh['item'=16,'code'=8] {'code'}, use_global_device_ids=true, to_apply=%region_20.21 | all-reduce | flops 4096 | bytes 32768 | tf_op jit(solution)/shard_map/psum | solution.py:81
  629.1 15.3 %add_reduce_fusion.2 = f32[8,8,16,64]{3,2,1,0:T(8,128)S(1)} fusion(f32[8,8,16,64,64]{3,4,2,1,0:T(8,128)} %get-tuple-element.105, f32[8,8,64]{2,1,0:T(8,128)S(1)} %add.163), kind=kLoop, calls=%fused_computation.34 | loop fusion | flops 8323072 | bytes 17055744 | tf_op jit(solution)/shard_map/reduce_max | solution.py:87
  644.4 20.7 %exponential_reduce_fusion.2 = f32[8,8,16,64]{3,2,1,0:T(8,128)S(1)} fusion(f32[8,8,16,64,64]{3,4,2,1,0:T(8,128)} %get-tuple-element.105, f32[8,8,16,64]{3,2,1,0:T(8,128)S(1)} %add_reduce_fusion.2, f32[8,8,64]{2,1,0:T(8,128)S(1)} %add.163), kind=kLoop, calls=%fused_computation.28 | loop fusion | flops 12517376 | bytes 17317888 | tf_op jit(solution)/shard_map/reduce_sum | solution.py:88
  665.0 13.3 %while.45 = (s32[]{:T(128)}, f32[128,64]{0,1:T(8,128)S(1)}, pred[4,256,128]{2,1,0:T(8,128)(4,1)S(1)}, f32[4,256,64]{2,1,0:T(8,128)S(1)}, s32[]{:T(128)}, /*index=5*/s32[]{:T(128)}) while((s32[]{:T(128)}, f32[128,64]{0,1:T(8,128)S(1)}, pred[4,256,128]{2,1,0:T(8,128)(4,1)S(1)}, f32[4,256,64]{2,1,0:T(8,128)S(1)}, s32[]{:T(128)}, ...), condition=%wide.region_24.25_spmd.clone, body=%wide.region_22.24_spmd.clone.sunk | while | flops 4202499 | bytes 426071 | solution.py:101
  682.3 69.6 %pmax.45 = f32[8192]{0:T(1024)S(1)} all-reduce(f32[8192]{0:T(1024)S(1)} %reshape.221), channel_id=1, replica_groups=mesh['item'=16,'code'=8] {'item'}, use_global_device_ids=true, to_apply=%region_25.26 | all-reduce | flops 8192 | bytes 65536 | tf_op jit(solution)/shard_map/pmax | solution.py:118
  751.9 69.5 %psum.61 = f32[8192]{0:T(1024)S(1)} all-reduce(f32[8192]{0:T(1024)S(1)} %exponential_multiply_fusion.1), channel_id=1, replica_groups=mesh['item'=16,'code'=8] {'item'}, use_global_device_ids=true, to_apply=%region_27.28 | all-reduce | flops 8192 | bytes 65536 | tf_op jit(solution)/shard_map/psum | solution.py:119
  848.3 23.5 %pmax.46 = f32[4096]{0:T(1024)S(1)} all-reduce(f32[4096]{0:T(1024)S(1)} %reshape.226), channel_id=1, replica_groups=mesh['item'=16,'code'=8] {'code'}, use_global_device_ids=true, to_apply=%region_29.30 | all-reduce | flops 4096 | bytes 32768 | tf_op jit(solution)/shard_map/pmax | solution.py:80
  871.8 23.8 %psum.62 = f32[4096]{0:T(1024)S(1)} all-reduce(f32[4096]{0:T(1024)S(1)} %exponential_multiply_fusion.3), channel_id=1, replica_groups=mesh['item'=16,'code'=8] {'code'}, use_global_device_ids=true, to_apply=%region_31.32 | all-reduce | flops 4096 | bytes 32768 | tf_op jit(solution)/shard_map/psum | solution.py:81
  895.7 15.3 %add_reduce_fusion = f32[8,8,16,64]{3,2,1,0:T(8,128)S(1)} fusion(f32[8,8,16,64,64]{3,4,2,1,0:T(8,128)} %get-tuple-element.105, f32[8,8,64]{2,1,0:T(8,128)S(1)} %add.171), kind=kLoop, calls=%fused_computation.32 | loop fusion | flops 8323072 | bytes 17055744 | tf_op jit(solution)/shard_map/reduce_max | solution.py:87
  911.0 20.7 %exponential_reduce_fusion = f32[8,8,16,64]{3,2,1,0:T(8,128)S(1)} fusion(f32[8,8,16,64,64]{3,4,2,1,0:T(8,128)} %get-tuple-element.105, f32[8,8,16,64]{3,2,1,0:T(8,128)S(1)} %add_reduce_fusion, f32[8,8,64]{2,1,0:T(8,128)S(1)} %add.171), kind=kLoop, calls=%fused_computation.26 | loop fusion | flops 12517376 | bytes 17317888 | tf_op jit(solution)/shard_map/reduce_sum | solution.py:88
  931.7 13.3 %while.46 = (s32[]{:T(128)}, f32[128,64]{0,1:T(8,128)S(1)}, pred[4,256,128]{2,1,0:T(8,128)(4,1)S(1)}, f32[4,256,64]{2,1,0:T(8,128)S(1)}, s32[]{:T(128)}, /*index=5*/s32[]{:T(128)}) while((s32[]{:T(128)}, f32[128,64]{0,1:T(8,128)S(1)}, pred[4,256,128]{2,1,0:T(8,128)(4,1)S(1)}, f32[4,256,64]{2,1,0:T(8,128)S(1)}, s32[]{:T(128)}, ...), condition=%wide.region_35.36_spmd.clone, body=%wide.region_33.35_spmd.clone.sunk | while | flops 4202499 | bytes 426071 | solution.py:101
  948.9 69.6 %pmax.47 = f32[8192]{0:T(1024)S(1)} all-reduce(f32[8192]{0:T(1024)S(1)} %reshape.228), channel_id=1, replica_groups=mesh['item'=16,'code'=8] {'item'}, use_global_device_ids=true, to_apply=%region_36.37 | all-reduce | flops 8192 | bytes 65536 | tf_op jit(solution)/shard_map/pmax | solution.py:118
  1018.5 69.5 %psum.63 = f32[8192]{0:T(1024)S(1)} all-reduce(f32[8192]{0:T(1024)S(1)} %exponential_multiply_fusion), channel_id=1, replica_groups=mesh['item'=16,'code'=8] {'item'}, use_global_device_ids=true, to_apply=%region_38.39 | all-reduce | flops 8192 | bytes 65536 | tf_op jit(solution)/shard_map/psum | solution.py:119
  (193 shorter events, 306.6 us)
Async XLA Ops:
  7.2 51.8 %all-gather.5.cloned.1.call-start = ((), (), s32[]{:S(2)}) async-start(), calls=%async_computation.1 | async-start | bytes 4718592 | tf_op jit(solution)/shard_map/all_gather | solution.py:17
  7.9 109.4 %all-gather.3.cloned.1.call-start = ((), (), s32[]{:S(2)}) async-start(), calls=%async_computation | async-start | bytes 8912896 | tf_op jit(solution)/shard_map/all_gather | solution.py:18
  285.0 74.0 %copy-start.3 = (f32[4096]{0:T(1024)S(1)}, f32[4096]{0:T(1024)}, u32[]{:S(2)}) copy-start(f32[4096]{0:T(1024)} %param.15) | copy-start | bytes 49156
  359.1 195.9 %copy-start.2 = (f32[8192]{0:T(1024)S(1)}, f32[8192]{0:T(1024)}, u32[]{:S(2)}) copy-start(f32[8192]{0:T(1024)} %param.16) | copy-start | bytes 98308
  629.1 36.0 %copy-start.1 = (f32[128,64]{0,1:T(8,128)S(1)}, f32[128,64]{0,1:T(8,128)}, u32[]{:S(2)}) copy-start(f32[128,64]{0,1:T(8,128)} %custom-call.1) | copy-start | bytes 98308
  895.6 36.1 %copy-start.4 = (f32[4096]{0:T(1024)}, f32[4096]{0:T(1024)S(1)}, u32[]{:S(2)}) copy-start(f32[4096]{0:T(1024)S(1)} %add_subtract_fusion.3) | copy-start | bytes 49156
  895.7 36.0 %copy-start = (f32[128,64]{0,1:T(8,128)S(1)}, f32[128,64]{0,1:T(8,128)}, u32[]{:S(2)}) copy-start(f32[128,64]{0,1:T(8,128)} %custom-call.2) | copy-start | bytes 98308
Sparse Core Ops, SparseCore 0:
  9.7 34.5 all-gather.4
  46.4 70.8 all-gather.2
where the time goes:
time: 1100 us
  blocking collectives  607 us (55%)
  other arithmetic  222 us (20%)
  local copies, waits for them, and re-layouts  101 us (9%)
  matrix products  89.9 us (8%)
  waiting for transfers between devices  54.1 us (5%)
  between operations  15.8 us (1%)
    pmax x3, blocking collectives, body(): joined_peak = lax.pmax(col_peak, 'item')  212 us
    psum x3, blocking collectives, body(): joined_total = lax.psum(col_total * jnp.exp(col_peak - joined_peak), 'item')  209 us
    dot_general x8, matrix products, build_tiles(): jnp.einsum('rbi,rbsj->bsij', own, picked, precision=lax.Precision.HIGHEST)  87.6 us
    pmax x3, blocking collectives, body(): merged_peak = lax.pmax(row_peak, 'code')  72.6 us
    psum x3, blocking collectives, body(): merged_total = lax.psum(row_total * jnp.exp(row_peak - merged_peak), 'code')  71.9 us
    reduce_sum x3, other arithmetic, col_reduce(): block_total = jnp.sum(jnp.exp(logits - block_peak[:, :, None, :]), axis=2)  62 us
    gather x8, local copies, waits for them, and re-layouts, build_tiles(): picked = code_column_splits[:, ids, :]  61.3 us
    all_gather x1, waiting for transfers between devices, body(): code_cols = lax.all_gather(codebook, 'item', axis=0, tiled=True)  52.7 us
  transfers between devices with their start and end apart: 2, of which 1 were waited for; matrix products, arithmetic and copies ran while one was open for 1% of the time, Pallas kernels for 0%

commit v1 on v0

v1 whole, which is shorter than its diff:
```python
import functools
import math

import jax
import jax.numpy as jnp
from jax import lax
from jax.experimental import pallas as pl
from jax.experimental.pallas import tpu as pltpu
from jax.sharding import PartitionSpec as P

BLOCK = 64
SLOTS = 8
KP = SLOTS // 2
NEG = -1e30
SOFTNESS = 0.1
MESH = pl.DeviceIdType.MESH
HIGHEST = lax.Precision.HIGHEST


def kernel(
    cb_ref,
    res_ref,
    wt_ref,
    cap_ref,
    tgt_ref,
    tgtt_ref,
    ids_ref,
    fout_ref,
    gout_ref,
    cg,
    rg,
    vh,
    vl,
    rt,
    s_ref,
    tm_ref,
    ts_ref,
    xrow,
    xy,
    xz,
    csend,
    crecv,
    rsend,
    rrecv,
    lsem,
    rowsend,
    rowrecv,
    ysend,
    yrecv,
    zsend,
    zrecv,
):
    item = lax.axis_index("item")
    code = lax.axis_index("code")
    z, y = item // 4, item % 4
    x, core = code // 2, code % 2
    cd = cg.shape[3]
    idv = rg.shape[2]
    width = 256
    scale = 1.0 / (SOFTNESS * math.sqrt(width))

    def at(zz, yy):
        return {"item": (zz % 4) * 4 + yy % 4, "code": code}

    def ac(cc):
        return {"item": item, "code": cc}

    bar = pltpu.get_barrier_semaphore()
    for d in range(1, 4):
        pl.semaphore_signal(bar, inc=1, device_id=at(z, y + d), device_id_type=MESH)
        pl.semaphore_signal(bar, inc=1, device_id=at(z + d, y), device_id_type=MESH)
    for d in range(1, 8):
        pl.semaphore_signal(bar, inc=1, device_id=ac((code + d) % 8), device_id_type=MESH)
    pl.semaphore_wait(bar, 13)

    half = cd // 2
    LO, HI = slice(0, half), slice(half, cd)
    sends = []

    def put(src, dst, ss, rs, dev):
        c = pltpu.make_async_remote_copy(
            src_ref=src, dst_ref=dst, send_sem=ss, recv_sem=rs, device_id=dev, device_id_type=MESH
        )
        c.start()
        sends.append(c)
        return c

    def place(h, p, s):
        zz, yy = (s, p) if h == 0 else (p, s)
        return (zz % 4) * 4 + yy % 4

    def where_to(h, p, s):
        zz, yy = (s, p) if h == 0 else (p, s)
        return at(zz, yy)

    pos = [(y, z), (z, y)]
    cnt = [0]

    def piece(h, p, s, cols=None, own=False):
        if own:
            return cb_ref.at[h]
        d = place(h, p, s)
        if cols is None:
            return cg.at[d, h]
        return cg.at[d, h, :, pl.ds(cols.start, cols.stop - cols.start)]

    def cput(h, src_ps, cols, to, own=False):
        i = cnt[0]
        cnt[0] += 1
        src = piece(h, *src_ps, cols, own)
        dst = piece(h, *src_ps, cols)
        return put(src, dst, csend.at[i], crecv.at[i], where_to(h, *to))

    prim, sec = {}, {}
    locals_ = []
    for h in range(2):
        p, s = pos[h]
        prim[h, 1] = cput(h, (p, s), None, (p + 1, s), True)
        prim[h, -1] = cput(h, (p, s), None, (p - 1, s), True)
        sec[h, 0, 1] = cput(h, (p, s), None, (p, s + 1), True)
        sec[h, 0, -1] = cput(h, (p, s), None, (p, s - 1), True)
        lc = pltpu.make_async_copy(cb_ref.at[h], cg.at[item, h], lsem.at[h])
        lc.start()
        locals_.append(lc)

    rhalf = idv // 2
    rcnt = [0]

    def rdev(xx):
        return (xx % 4) * 2 + core

    def rput(xx, cols, to, own=False):
        i = rcnt[0]
        rcnt[0] += 1
        d = rdev(xx)
        if cols is None:
            dst = rg.at[d]
        else:
            dst = rg.at[d, :, pl.ds(cols * rhalf, rhalf)]
        return put(res_ref if own else dst, dst, rsend.at[i], rrecv.at[i], ac(to))

    other = x * 2 + (1 - core)
    rp = {}
    rp[1] = rput(x, None, rdev(x + 1), True)
    rp[-1] = rput(x, None, rdev(x - 1), True)
    rc = [rput(x, None, other, True)]
    lc = pltpu.make_async_copy(res_ref, rg.at[code], lsem.at[2])
    lc.start()
    locals_.append(lc)

    ph, sh = {}, {}
    for d in (1, -1):
        for h in range(2):
            p, s = pos[h]
            prim[h, d].wait_recv()
            ph[h, d] = cput(h, (p - d, s), LO if d > 0 else HI, (p + d, s))
            sec[h, d, 1] = cput(h, (p - d, s), None, (p, s + 1))
            sec[h, d, -1] = cput(h, (p - d, s), None, (p, s - 1))
        rp[d].wait_recv()
        rp[2 * d] = rput(x - d, 0 if d > 0 else 1, rdev(x + d))
        rc.append(rput(x - d, None, other))
        for h in range(2):
            p, s = pos[h]
            sec[h, 0, d].wait_recv()
            sh[h, 0, d] = cput(h, (p, s - d), LO if d > 0 else HI, (p, s + d))
    for h in range(2):
        p, s = pos[h]
        ph[h, 1].wait_recv()
        ph[h, -1].wait_recv()
        sec[h, 2, 1] = cput(h, (p + 2, s), None, (p, s + 1))
        sec[h, 2, -1] = cput(h, (p + 2, s), None, (p, s - 1))
    rp[2].wait_recv()
    rp[-2].wait_recv()
    rc.append(rput(x + 2, None, other))
    offs = {0: 0, 1: -1, -1: 1, 2: 2}
    for k in (1, -1, 2):
        for d in (1, -1):
            for h in range(2):
                p, s = pos[h]
                sec[h, k, d].wait_recv()
                sh[h, k, d] = cput(h, (p + offs[k], s - d), LO if d > 0 else HI, (p, s + d))
    for c in rc:
        c.wait_recv()
    for c in locals_:
        c.wait()

    lane = lax.broadcasted_iota(jnp.int32, (1, 128), 1)
    left = lane < 64

    def split_items(c, carry):
        col = pl.ds(pl.multiple_of(c * 128, 128), 128)
        v = rg[:, :, col].reshape(width, 128).T
        hi = v.astype(jnp.bfloat16)
        lo = (v - hi.astype(jnp.float32)).astype(jnp.bfloat16)
        for b in range(2):
            rt[2 * c + b, 0:64, :] = hi[b * 64 : b * 64 + 64]
            rt[2 * c + b, 64:128, :] = lo[b * 64 : b * 64 + 64]
        return carry

    lax.fori_loop(0, idv // 128, split_items, 0)

    for k in (0, 1, -1, 2):
        for d in (1, -1):
            for h in range(2):
                sh[h, k, d].wait_recv()

    def split_codes(q, carry):
        col = pl.ds(pl.multiple_of(q * 128, 128), 128)
        v = cg[:, :, :, col].reshape(width, 128)
        w = pltpu.roll(v, 64, 1)
        for b, t in ((0, v), (1, w)):
            hi = t.astype(jnp.bfloat16)
            vh[2 * q + b] = hi
            vl[2 * q + b] = (t - hi.astype(jnp.float32)).astype(jnp.bfloat16)
        return carry

    lax.fori_loop(0, cd // 128, split_codes, 0)

    lane64 = lax.broadcasted_iota(jnp.int32, (64, 128), 1)
    leftw = lax.broadcasted_iota(jnp.int32, (width, 128), 1) < 64

    def rows_at(k, b):
        return pl.ds(k * 64 + b, 1)

    def column(f, b):
        return jnp.sum(jnp.where(lane64 == b, f, 0.0), axis=1, keepdims=True)

    def score_block(b, acc):
        wh, wl = [], []
        for k in range(KP):
            i0 = ids_ref[b, 2 * k]
            i1 = ids_ref[b, 2 * k + 1]
            wh.append(jnp.where(leftw, vh[i0], vh[i1]))
            wl.append(jnp.where(leftw, vl[i0], vl[i1]))
        wh = jnp.concatenate(wh, axis=1)
        wl = jnp.concatenate(wl, axis=1)
        a = rt[b]
        d1 = jnp.dot(a, wh, preferred_element_type=jnp.float32)
        d2 = jnp.dot(a[0:64], wl, preferred_element_type=jnp.float32)
        s = (d1[0:64] + (d1[64:128] + d2)) * scale
        live = jnp.concatenate([tgt_ref[rows_at(k, b), :] for k in range(KP)], axis=1) >= 0
        s = jnp.where(live, s, NEG)
        s_ref[b] = s
        m = jnp.max(s, axis=1, keepdims=True)
        t = jnp.sum(jnp.exp(s - m), axis=1, keepdims=True)
        return jnp.where(lane64 == b, m + jnp.log(t), acc)

    row = lax.fori_loop(0, 64, score_block, jnp.zeros((64, 128), jnp.float32))

    lane32 = lax.broadcasted_iota(jnp.int32, (32, 128), 1) < 64

    def pack(r):
        return jnp.where(lane32, r[0:32], pltpu.roll(r[32:64], 64, 1))

    def unpack(m):
        return jnp.concatenate([m, pltpu.roll(m, 64, 1)], axis=0)

    def lse(parts):
        m = functools.reduce(jnp.maximum, parts)
        t = functools.reduce(jnp.add, [jnp.exp(q - m) for q in parts])
        return m + jnp.log(t)

    def total(parts):
        return functools.reduce(jnp.add, parts)

    def row_exchange(n, r, extra, merge):
        xrow[n, code, 0:32, :] = pack(r)
        size = 32
        if extra is not None:
            xrow[n, code, 32:40, :] = jnp.broadcast_to(extra, (8, 128))
            size = 40
        cs = []
        for d in range(1, 8):
            ref = xrow.at[n, code, pl.ds(0, size), :]
            i = n * 7 + d - 1
            cs.append(put(ref, ref, rowsend.at[i], rowrecv.at[i], ac((code + d) % 8)))
        for c in cs:
            c.wait_recv()
        out = unpack(merge([xrow[n, q, 0:32, :] for q in range(8)]))
        if extra is None:
            return out
        return out, total([xrow[n, q, 32:40, :] for q in range(8)])[0:1, 0:1]

    def one_axis(n, buf, me, ssem, rsem, dev, val, extra, merge):
        buf[n, me, 0:64, :] = val
        size = 64
        if extra is not None:
            buf[n, me, 64:72, :] = jnp.broadcast_to(extra, (8, 128))
            size = 72
        cs = []
        for d in range(1, 4):
            ref = buf.at[n, me, pl.ds(0, size), :]
            i = n * 3 + d - 1
            cs.append(put(ref, ref, ssem.at[i], rsem.at[i], dev(d)))
        for c in cs:
            c.wait_recv()
        out = merge([buf[n, q, 0:64, :] for q in range(4)])
        if extra is None:
            return out, None
        return out, total([buf[n, q, 64:72, :] for q in range(4)])[0:1, 0:1]

    def col_exchange(n, val, extra, merge):
        val, extra = one_axis(n, xy, y, ysend, yrecv, lambda d: at(z, y + d), val, extra, merge)
        return one_axis(n, xz, z, zsend, zrecv, lambda d: at(z + d, y), val, extra, merge)

    wt = wt_ref[...]
    cap = cap_ref[...]
    wsum = jnp.sum(jnp.where(lane64 < 64, wt, 0.0), keepdims=True)
    csum = jnp.sum(cap, keepdims=True)
    row, capacity = row_exchange(0, row, csum, lse)
    f1 = jnp.log(wt) - row

    def col_first(b, carry):
        c = s_ref[b] + column(f1, b)
        m = jnp.max(c, axis=0, keepdims=True)
        t = jnp.sum(jnp.exp(c - m), axis=0, keepdims=True)
        for k in range(KP):
            tm_ref[rows_at(k, b), :] = m[:, k * 128 : k * 128 + 128]
            ts_ref[rows_at(k, b), :] = t[:, k * 128 : k * 128 + 128]
        return carry

    lax.fori_loop(0, 64, col_first, 0)

    block = lax.broadcasted_iota(jnp.int32, (128, 128), 0)

    def spread_max(r, acc):
        for u in range(4):
            one = pl.ds(r * 4 + u, 1)
            acc = jnp.maximum(acc, jnp.where(block == tgt_ref[one, :], tm_ref[one, :], NEG))
        return acc

    peak = lax.fori_loop(0, 64, spread_max, jnp.full((128, 128), NEG, jnp.float32))
    peak = jnp.maximum(peak, pltpu.roll(peak, 64, 1))

    lanes = lax.broadcasted_iota(jnp.int32, (256, 128), 1)
    tgt = tgt_ref[...]
    hot_even = jnp.where(lanes == tgt[:, 0:1], 1.0, 0.0)
    hot_odd = jnp.where(lanes == tgt[:, 64:65], 1.0, 0.0)
    sub = lax.broadcasted_iota(jnp.int32, (128, 256), 0)
    hot_even_t = jnp.where(sub == tgtt_ref[0], 1.0, 0.0)
    hot_odd_t = jnp.where(sub == tgtt_ref[1], 1.0, 0.0)

    def dot(a, b):
        return jnp.dot(a, b, precision=HIGHEST, preferred_element_type=jnp.float32)

    def spread_out(v):
        return jnp.where(left, dot(hot_even, v), dot(hot_odd, v))

    def collect(v):
        o = dot(hot_even_t, jnp.where(left, v, 0.0)) + dot(hot_odd_t, jnp.where(left, 0.0, v))
        return o + pltpu.roll(o, 64, 1)

    def compact(v):
        return jnp.where(left, v[0:64], v[64:128])

    def expand(c):
        r = pltpu.roll(c, 64, 1)
        return jnp.concatenate([jnp.where(left, c, r), jnp.where(left, r, c)], axis=0)

    tiles = ts_ref[...] * jnp.exp(tm_ref[...] - spread_out(peak))
    sums = collect(tiles)
    some = sums > 0.0
    col = jnp.where(some, peak + jnp.log(jnp.where(some, sums, 1.0)), NEG)
    col, weight = col_exchange(0, compact(col), wsum, lse)
    lw = jnp.log(weight)
    f1 = f1 - lw
    g1 = jnp.log(cap) - jnp.log(capacity) - (col - lw)
    amass = wt / weight
    bmass = cap / capacity

    tm_ref[...] = spread_out(expand(g1))

    def first_rows(b, acc):
        g = jnp.concatenate([tm_ref[rows_at(k, b), :] for k in range(KP)], axis=1)
        e = jnp.exp(s_ref[b] + column(f1, b) + g)
        s_ref[b] = e
        return jnp.where(lane64 == b, jnp.sum(e, axis=1, keepdims=True), acc)

    row = lax.fori_loop(0, 64, first_rows, jnp.ones((64, 128), jnp.float32))
    u = amass / row_exchange(1, row, None, total)

    def cols(u):
        def body(b, carry):
            t = jnp.sum(s_ref[b] * column(u, b), axis=0, keepdims=True)
            for k in range(KP):
                ts_ref[rows_at(k, b), :] = t[:, k * 128 : k * 128 + 128]
            return carry

        lax.fori_loop(0, 64, body, 0)
        return compact(collect(ts_ref[...]))

    v = bmass / col_exchange(1, cols(u), None, total)[0]

    tm_ref[...] = spread_out(expand(v))

    def rows(b, acc):
        g = jnp.concatenate([tm_ref[rows_at(k, b), :] for k in range(KP)], axis=1)
        return jnp.where(lane64 == b, jnp.sum(s_ref[b] * g, axis=1, keepdims=True), acc)

    row = lax.fori_loop(0, 64, rows, jnp.ones((64, 128), jnp.float32))
    u = amass / row_exchange(2, row, None, total)
    fout_ref[...] = f1 + jnp.log(u)
    v = bmass / col_exchange(2, cols(u), None, total)[0]
    gout_ref[...] = g1 + jnp.log(v)

    for c in sends:
        c.wait_send()


def body(residuals, codebook, item_weight, code_capacity, pairs):
    items = residuals.shape[1]
    codes = codebook.shape[1]
    nb = items // BLOCK
    live = pairs >= 0
    slot = jnp.arange(pairs.shape[1], dtype=jnp.int32)
    rank = jnp.sum(live[:, None, :] & (slot[None, None, :] < slot[None, :, None]), axis=2)
    pick = live[:, None, :] & (rank[:, None, :] == jnp.arange(SLOTS, dtype=jnp.int32)[None, :, None])
    tgt = jnp.sum(jnp.where(pick, pairs[:, None, :] + 1, 0), axis=2) - 1
    flip = jnp.arange(SLOTS, dtype=jnp.int32) & 1
    ids = jnp.bitwise_xor(jnp.maximum(tgt, 0), flip[None, :])
    by_pair = tgt.T.reshape(KP, 2, nb)
    tgtt = by_pair.transpose(1, 0, 2).reshape(2, 1, KP * nb)
    tgtrow = jnp.repeat(by_pair.transpose(0, 2, 1).reshape(KP * nb, 2), 64, axis=1)
    wt = jnp.pad(item_weight.reshape(nb, BLOCK).T, ((0, 0), (0, 128 - nb)), constant_values=1.0)
    cap = code_capacity.reshape(2, 64, BLOCK).transpose(1, 0, 2).reshape(64, 128)
    vm = pl.BlockSpec(memory_space=pltpu.VMEM)
    hbm = pl.BlockSpec(memory_space=pl.ANY)
    f32, bf16 = jnp.float32, jnp.bfloat16
    dma = pltpu.SemaphoreType.DMA
    f, g = pl.pallas_call(
        kernel,
        out_shape=[jax.ShapeDtypeStruct((64, 128), f32), jax.ShapeDtypeStruct((64, 128), f32)],
        in_specs=[hbm, hbm, vm, vm, vm, vm, pl.BlockSpec(memory_space=pltpu.SMEM)],
        out_specs=[vm, vm],
        scratch_shapes=[
            pltpu.VMEM((16, 2, 8, codes), f32),
            pltpu.VMEM((8, 32, items), f32),
            pltpu.VMEM((128, 256, 128), bf16),
            pltpu.VMEM((128, 256, 128), bf16),
            pltpu.VMEM((64, 128, 256), bf16),
            pltpu.VMEM((64, 64, 512), f32),
            pltpu.VMEM((256, 128), f32),
            pltpu.VMEM((256, 128), f32),
            pltpu.VMEM((3, 8, 40, 128), f32),
            pltpu.VMEM((3, 4, 72, 128), f32),
            pltpu.VMEM((3, 4, 72, 128), f32),
            dma((40,)),
            dma((40,)),
            dma((8,)),
            dma((8,)),
            dma((3,)),
            dma((21,)),
            dma((21,)),
            dma((9,)),
            dma((9,)),
            dma((9,)),
            dma((9,)),
        ],
        compiler_params=pltpu.CompilerParams(
            collective_id=0, has_side_effects=True, vmem_limit_bytes=60 * 1024 * 1024
        ),
    )(codebook.reshape(2, 8, codes), residuals, wt, cap, tgtrow, tgtt, ids)
    f = f[:, :nb].T.reshape(items)
    g = g.reshape(64, 2, BLOCK).transpose(1, 0, 2).reshape(codes)
    return f, g


def solution(mesh):
    placed = (P("code", "item"), P("item", "code"), P("item"), P("code"), P("item", "code"))
    return jax.shard_map(
        body, mesh=mesh, in_specs=placed, out_specs=(P("item"), P("code")), check_vma=False
    )
```

time: 1100 us -> 178 us (0.16)
  blocking collectives: 607 us -> 0 us
  other arithmetic: 222 us -> 1.49 us
  Pallas kernels: 0 us -> 169 us
  local copies, waits for them, and re-layouts: 101 us -> 6.24 us
  matrix products: 89.9 us -> 0 us
  waiting for transfers between devices: 54.1 us -> 0 us
  between operations: 15.8 us -> 0.71 us
    psum x7 -> x0, blocking collectives: 323 us -> none  [the longest x3 209 us: body(): joined_total = lax.psum(col_total * jnp.exp(col_peak - joined_peak), 'item')]
    pmax x6 -> x0, blocking collectives: 284 us -> none  [the longest x3 212 us: body(): joined_peak = lax.pmax(col_peak, 'item')]
    pallas_call x0 -> x1, Pallas kernels: none -> 169 us  [body(): pl.pallas_call(kernel, out_shape=[jax.ShapeDtypeStruct((64, 128), f32), j...]
    reduce_max x18 -> x0, other arithmetic: 120 us -> none  [the longest x3 45.9 us: col_reduce(): block_peak = jnp.max(logits, axis=2)]
    reduce_sum x8 -> x2, other arithmetic: 100 us -> 0.14 us  [the longest x1 0.11 us: body(): jnp.sum(live[:, None, :] & (slot[None, None, :] < slot[None, :, None]), a...]
    dot_general x11 -> x0, matrix products: 89.9 us -> none  [the longest x8 87.6 us: build_tiles(): jnp.einsum('rbi,rbsj->bsij', own, picked, precision=lax.Precision.HIGHEST)]
    gather x14 -> x0, local copies, waits for them, and re-layouts: 78.1 us -> none  [the longest x8 61.3 us: build_tiles(): picked = code_column_splits[:, ids, :]]
    all_gather x2 -> x0, waiting for transfers between devices: 52.7 us -> none  [the longest x1 52.7 us: body(): code_cols = lax.all_gather(codebook, 'item', axis=0, tiled=True)]
  transfers between devices with their start and end apart: 2 -> 0, of which waited for: 1 -> 0; matrix products, arithmetic and copies ran while one was open for 1% -> 0% of each run, Pallas kernels for 0% -> 0%
where the time goes in v1:
time: 178 us
  Pallas kernels  169 us (95%)
  local copies, waits for them, and re-layouts  6.24 us (4%)
    pallas_call x1, Pallas kernels, body(): pl.pallas_call(kernel, out_shape=[jax.ShapeDtypeStruct((64, 128), f32), j...  169 us

profile of v1, /device:TPU:0, one launch (start us, length us, event | category | flops | bytes accessed | tf_op | source)
XLA Modules:
  0.0 177.6 jit_solution(2031185042934589219)
XLA Ops:
  0.6 0.7 broadcast_compare_fusion
  1.3 0.1 convert_reduce_fusion
  1.5 0.6 copy-done.1
  2.1 0.1 copy.33
  2.2 0.6 maximum_xor_fusion
  2.8 0.1 copy.35
  2.8 0.1 reshape.65
  3.0 0.0 copy-start
  3.0 0.8 copy.38.tgt_ref
  3.7 0.7 reshape.67.tgtt_ref
  4.4 0.1 reshape.62
  4.5 0.1 copy.32
  4.5 0.0 copy-start.3
  4.5 0.7 reshape.63.cap_ref
  5.2 0.0 copy-done.3
  5.2 0.1 reshape.61
  5.3 0.1 copy.31
  5.4 0.6 pad.4.wt_ref
  6.0 169.2 %shard_map.68 = (f32[64,128]{1,0:T(8,128)}, f32[64,128]{1,0:T(8,128)}) custom-call(f32[2,8,8192]{2,1,0:T(8,128)} %bitcast.18, f32[32,4096]{1,0:T(8,128)} %res_ref.1, f32[64,128]{1,0:T(8,128)} %pad.4.wt_ref, f32[64,128]{1,0:T(8,128)} %reshape.63.cap_ref, s32[256,128]{1,0:T(8,128)} %copy.38.tgt_ref, s32[2,1,256]{2,1,0:T(1,128)} %reshape.67.tgtt_ref, ...), custom_call_target="tpu_custom_call" | custom-call | tf_op jit(solution)/shard_map/pallas_call | solution.py:430
  175.2 0.9 reshape.69
  176.1 0.7 reshape.70
  176.8 0.1 copy-done.2
  176.8 0.1 copy.39
  176.9 0.7 reshape.68
  (12 shorter events, 0.1 us)
Async XLA Ops:
  1.3 0.7 copy-start.1
  3.0 1.4 copy-start
  4.5 0.7 copy-start.3
  176.1 0.8 copy-start.2

commit v2 on v1

--- a/solution.py
+++ b/solution.py
@@ -14,7 +14,6 @@
 NEG = -1e30
 SOFTNESS = 0.1
 MESH = pl.DeviceIdType.MESH
-HIGHEST = lax.Precision.HIGHEST
 
 
 def kernel(
@@ -22,9 +21,7 @@
     res_ref,
     wt_ref,
     cap_ref,
-    tgt_ref,
-    tgtt_ref,
-    ids_ref,
+    pairs_ref,
     fout_ref,
     gout_ref,
     cg,
@@ -33,6 +30,10 @@
     vl,
     rt,
     s_ref,
+    padded,
+    tgt_ref,
+    ids_v,
+    ids_ref,
     tm_ref,
     ts_ref,
     xrow,
@@ -71,6 +72,30 @@
         pl.semaphore_signal(bar, inc=1, device_id=at(z + d, y), device_id_type=MESH)
     for d in range(1, 8):
         pl.semaphore_signal(bar, inc=1, device_id=ac((code + d) % 8), device_id_type=MESH)
+
+    lane = lax.broadcasted_iota(jnp.int32, (1, 128), 1)
+    left = lane < 64
+    lane64 = lax.broadcasted_iota(jnp.int32, (64, 128), 1)
+    padded[...] = jnp.full((64, 128), -1, jnp.int32)
+    padded[:, 0:16] = pairs_ref[...]
+    named = padded[...]
+    live = jnp.where(named >= 0, 1, 0)
+    count = live
+    for sh in (1, 2, 4, 8):
+        count = count + jnp.where(lane64 >= sh, pltpu.roll(count, sh, 1), 0)
+    count = live * count
+    picked = []
+    ids = jnp.zeros((64, 128), jnp.int32)
+    for k in range(SLOTS):
+        one = jnp.max(jnp.where(count == k + 1, named, -1), axis=1, keepdims=True)
+        ids = jnp.where(lane64 == k, jnp.maximum(one, 0) ^ (k & 1), ids)
+        picked.append(jnp.where(one < 0, -1, (one >> 1) + (one & 1) * 64))
+    for k in range(KP):
+        tgt_ref[k * 64 : k * 64 + 64, :] = jnp.where(left, picked[2 * k], picked[2 * k + 1])
+    ids_v[...] = ids
+    idc = pltpu.make_async_copy(ids_v, ids_ref, lsem.at[3])
+    idc.start()
+    idc.wait()
     pl.semaphore_wait(bar, 13)
 
     half = cd // 2
@@ -148,11 +173,51 @@
     lc.start()
     locals_.append(lc)
 
+    tasks = []
+    parts = {}
+
+    def split_items(c, carry):
+        col = pl.ds(pl.multiple_of(c * 128, 128), 128)
+        v = rg[:, :, col].reshape(width, 128).T * scale
+        hi = v.astype(jnp.bfloat16)
+        lo = (v - hi.astype(jnp.float32)).astype(jnp.bfloat16)
+        for b in range(2):
+            rt[2 * c + b, 0:64, :] = hi[b * 64 : b * 64 + 64]
+            rt[2 * c + b, 64:128, :] = lo[b * 64 : b * 64 + 64]
+        return carry
+
+    def split_codes(d):
+        def step(j, carry):
+            for r in range(8):
+                q = j * 8 + r
+                col = pl.ds(pl.multiple_of(q * 128, 128), 128)
+                v = cg[d, :, :, col].reshape(16, 128)
+                for b, t in ((0, v), (1, pltpu.roll(v, 64, 1))):
+                    hi = t.astype(jnp.bfloat16)
+                    vh[2 * q + b, d] = hi
+                    vl[2 * q + b, d] = (t - hi.astype(jnp.float32)).astype(jnp.bfloat16)
+            return carry
+
+        lax.fori_loop(0, cd // 1024, step, 0)
+
+    def got(h, op, os, share):
+        dy, dz = ((op, os) if h == 0 else (os, op))
+        key = dy % 4, dz % 4
+        parts[key] = parts.get(key, 0) + share
+        if parts[key] == 4:
+            d = ((z + dz) % 4) * 4 + (y + dy) % 4
+            tasks.append(lambda: split_codes(d))
+
+    def work(n):
+        for _ in range(min(n, len(tasks))):
+            tasks.pop(0)()
+
     ph, sh = {}, {}
     for d in (1, -1):
         for h in range(2):
             p, s = pos[h]
             prim[h, d].wait_recv()
+            got(h, -d, 0, 2)
             ph[h, d] = cput(h, (p - d, s), LO if d > 0 else HI, (p + d, s))
             sec[h, d, 1] = cput(h, (p - d, s), None, (p, s + 1))
             sec[h, d, -1] = cput(h, (p - d, s), None, (p, s - 1))
@@ -162,90 +227,97 @@
         for h in range(2):
             p, s = pos[h]
             sec[h, 0, d].wait_recv()
+            got(h, 0, -d, 2)
             sh[h, 0, d] = cput(h, (p, s - d), LO if d > 0 else HI, (p, s + d))
+    for c in locals_:
+        c.wait()
+    for h in range(2):
+        got(h, 0, 0, 2)
     for h in range(2):
         p, s = pos[h]
+        work(1)
         ph[h, 1].wait_recv()
         ph[h, -1].wait_recv()
+        got(h, 2, 0, 2)
         sec[h, 2, 1] = cput(h, (p + 2, s), None, (p, s + 1))
         sec[h, 2, -1] = cput(h, (p + 2, s), None, (p, s - 1))
     rp[2].wait_recv()
     rp[-2].wait_recv()
     rc.append(rput(x + 2, None, other))
     offs = {0: 0, 1: -1, -1: 1, 2: 2}
-    for k in (1, -1, 2):
+
+    def secondary(k):
         for d in (1, -1):
             for h in range(2):
                 p, s = pos[h]
+                work(1)
                 sec[h, k, d].wait_recv()
+                got(h, offs[k], -d, 2)
                 sh[h, k, d] = cput(h, (p + offs[k], s - d), LO if d > 0 else HI, (p, s + d))
+
+    def halves(k):
+        for d in (1, -1):
+            for h in range(2):
+                work(1)
+                sh[h, k, d].wait_recv()
+                got(h, offs[k], 2, 1)
+
+    secondary(1)
     for c in rc:
         c.wait_recv()
-    for c in locals_:
-        c.wait()
-
-    lane = lax.broadcasted_iota(jnp.int32, (1, 128), 1)
-    left = lane < 64
-
-    def split_items(c, carry):
-        col = pl.ds(pl.multiple_of(c * 128, 128), 128)
-        v = rg[:, :, col].reshape(width, 128).T
-        hi = v.astype(jnp.bfloat16)
-        lo = (v - hi.astype(jnp.float32)).astype(jnp.bfloat16)
-        for b in range(2):
-            rt[2 * c + b, 0:64, :] = hi[b * 64 : b * 64 + 64]
-            rt[2 * c + b, 64:128, :] = lo[b * 64 : b * 64 + 64]
-        return carry
-
-    lax.fori_loop(0, idv // 128, split_items, 0)
-
-    for k in (0, 1, -1, 2):
-        for d in (1, -1):
-            for h in range(2):
-                sh[h, k, d].wait_recv()
-
-    def split_codes(q, carry):
-        col = pl.ds(pl.multiple_of(q * 128, 128), 128)
-        v = cg[:, :, :, col].reshape(width, 128)
-        w = pltpu.roll(v, 64, 1)
-        for b, t in ((0, v), (1, w)):
-            hi = t.astype(jnp.bfloat16)
-            vh[2 * q + b] = hi
-            vl[2 * q + b] = (t - hi.astype(jnp.float32)).astype(jnp.bfloat16)
-        return carry
-
-    lax.fori_loop(0, cd // 128, split_codes, 0)
-
-    lane64 = lax.broadcasted_iota(jnp.int32, (64, 128), 1)
-    leftw = lax.broadcasted_iota(jnp.int32, (width, 128), 1) < 64
+    for g in range(8):
+        n = idv // 128 // 8
+        tasks.append(lambda g=g, n=n: lax.fori_loop(g * n, g * n + n, split_items, 0))
+    secondary(-1)
+    halves(0)
+    secondary(2)
+    for k in (1, -1, 2):
+        halves(k)
+    work(len(tasks))
+
+    UN = 4
 
     def rows_at(k, b):
         return pl.ds(k * 64 + b, 1)
 
+    def home(b):
+        return (b & 1) * 32 + (b >> 1)
+
     def column(f, b):
-        return jnp.sum(jnp.where(lane64 == b, f, 0.0), axis=1, keepdims=True)
+        return jnp.sum(jnp.where(lane64 == home(b), f, 0.0), axis=1, keepdims=True)
+
+    def ks(k):
+        return slice(k * 128, k * 128 + 128)
+
+    def blocks(body, init, un=UN):
+        def step(j, acc):
+            for r in range(un):
+                acc = body(j * un + r, acc)
+            return acc
+
+        return lax.fori_loop(0, 64 // un, step, init)
 
     def score_block(b, acc):
-        wh, wl = [], []
+        a = rt[b]
+        ss = []
         for k in range(KP):
             i0 = ids_ref[b, 2 * k]
             i1 = ids_ref[b, 2 * k + 1]
-            wh.append(jnp.where(leftw, vh[i0], vh[i1]))
-            wl.append(jnp.where(leftw, vl[i0], vl[i1]))
-        wh = jnp.concatenate(wh, axis=1)
-        wl = jnp.concatenate(wl, axis=1)
-        a = rt[b]
-        d1 = jnp.dot(a, wh, preferred_element_type=jnp.float32)
-        d2 = jnp.dot(a[0:64], wl, preferred_element_type=jnp.float32)
-        s = (d1[0:64] + (d1[64:128] + d2)) * scale
-        live = jnp.concatenate([tgt_ref[rows_at(k, b), :] for k in range(KP)], axis=1) >= 0
-        s = jnp.where(live, s, NEG)
-        s_ref[b] = s
-        m = jnp.max(s, axis=1, keepdims=True)
-        t = jnp.sum(jnp.exp(s - m), axis=1, keepdims=True)
-        return jnp.where(lane64 == b, m + jnp.log(t), acc)
-
-    row = lax.fori_loop(0, 64, score_block, jnp.zeros((64, 128), jnp.float32))
+            wh = jnp.concatenate([vh[i0].reshape(width, 128), vh[i1].reshape(width, 128)], axis=1)
+            wl = jnp.concatenate([vl[i0].reshape(width, 128), vl[i1].reshape(width, 128)], axis=1)
+            d1 = jnp.dot(a, wh, preferred_element_type=jnp.float32)
+            d2 = jnp.dot(a[0:64], wl, preferred_element_type=jnp.float32)
+            t = d1[0:64] + (d1[64:128] + d2)
+            s = jnp.where(left, t[:, 0:128], t[:, 128:256])
+            s = jnp.where(tgt_ref[rows_at(k, b), :] >= 0, s, NEG)
+            s_ref[b, :, ks(k)] = s
+            ss.append(s)
+        m = jnp.max(functools.reduce(jnp.maximum, ss), axis=1, keepdims=True)
+        t = functools.reduce(jnp.add, [jnp.exp(s - m) for s in ss])
+        t = jnp.sum(t, axis=1, keepdims=True)
+        return jnp.where(lane64 == home(b), m + jnp.log(t), acc)
+
+    row = blocks(score_block, jnp.zeros((64, 128), jnp.float32), 2)
 
     lane32 = lax.broadcasted_iota(jnp.int32, (32, 128), 1) < 64
 
@@ -303,7 +375,8 @@
         val, extra = one_axis(n, xy, y, ysend, yrecv, lambda d: at(z, y + d), val, extra, merge)
         return one_axis(n, xz, z, zsend, zrecv, lambda d: at(z + d, y), val, extra, merge)
 
-    wt = wt_ref[...]
+    turned = jnp.concatenate([wt_ref[...], jnp.ones((96, 128), jnp.float32)], axis=0).T
+    wt = jnp.where(lane64 < 32, turned[0:64], pltpu.roll(turned[64:128], 32, 1))
     cap = cap_ref[...]
     wsum = jnp.sum(jnp.where(lane64 < 64, wt, 0.0), keepdims=True)
     csum = jnp.sum(cap, keepdims=True)
@@ -311,15 +384,15 @@
     f1 = jnp.log(wt) - row
 
     def col_first(b, carry):
-        c = s_ref[b] + column(f1, b)
-        m = jnp.max(c, axis=0, keepdims=True)
-        t = jnp.sum(jnp.exp(c - m), axis=0, keepdims=True)
+        f = column(f1, b)
         for k in range(KP):
-            tm_ref[rows_at(k, b), :] = m[:, k * 128 : k * 128 + 128]
-            ts_ref[rows_at(k, b), :] = t[:, k * 128 : k * 128 + 128]
+            c = s_ref[b, :, ks(k)] + f
+            m = jnp.max(c, axis=0, keepdims=True)
+            tm_ref[rows_at(k, b), :] = m
+            ts_ref[rows_at(k, b), :] = jnp.sum(jnp.exp(c - m), axis=0, keepdims=True)
         return carry
 
-    lax.fori_loop(0, 64, col_first, 0)
+    blocks(col_first, 0)
 
     block = lax.broadcasted_iota(jnp.int32, (128, 128), 0)
 
@@ -334,20 +407,31 @@
 
     lanes = lax.broadcasted_iota(jnp.int32, (256, 128), 1)
     tgt = tgt_ref[...]
-    hot_even = jnp.where(lanes == tgt[:, 0:1], 1.0, 0.0)
-    hot_odd = jnp.where(lanes == tgt[:, 64:65], 1.0, 0.0)
-    sub = lax.broadcasted_iota(jnp.int32, (128, 256), 0)
-    hot_even_t = jnp.where(sub == tgtt_ref[0], 1.0, 0.0)
-    hot_odd_t = jnp.where(sub == tgtt_ref[1], 1.0, 0.0)
-
-    def dot(a, b):
-        return jnp.dot(a, b, precision=HIGHEST, preferred_element_type=jnp.float32)
+    hot = jnp.concatenate(
+        [jnp.where(lanes == tgt[:, 0:1], 1.0, 0.0), jnp.where(lanes == tgt[:, 64:65], 1.0, 0.0)], axis=1
+    )
+    hot_t = jnp.concatenate(
+        [hot[:, 0:128].T, hot[:, 128:256].T], axis=1
+    ).astype(jnp.bfloat16)
+    hot = hot.astype(jnp.bfloat16)
+
+    def hot_dot(one, v):
+        out = []
+        for _ in range(3):
+            h = v.astype(jnp.bfloat16).astype(jnp.float32)
+            out.append(h)
+            v = v - h
+        w = jnp.concatenate(out, axis=1)
+        side = (lax.broadcasted_iota(jnp.int32, (1, 384), 1) & 64) == 0
+        w = jnp.concatenate([jnp.where(side, w, 0.0), jnp.where(side, 0.0, w)], axis=0)
+        o = jnp.dot(one, w.astype(jnp.bfloat16), preferred_element_type=jnp.float32)
+        return o[:, 0:128] + (o[:, 128:256] + o[:, 256:384])
 
     def spread_out(v):
-        return jnp.where(left, dot(hot_even, v), dot(hot_odd, v))
+        return hot_dot(hot, v)
 
     def collect(v):
-        o = dot(hot_even_t, jnp.where(left, v, 0.0)) + dot(hot_odd_t, jnp.where(left, 0.0, v))
+        o = hot_dot(hot_t, v)
         return o + pltpu.roll(o, 64, 1)
 
     def compact(v):
@@ -371,22 +455,25 @@
     tm_ref[...] = spread_out(expand(g1))
 
     def first_rows(b, acc):
-        g = jnp.concatenate([tm_ref[rows_at(k, b), :] for k in range(KP)], axis=1)
-        e = jnp.exp(s_ref[b] + column(f1, b) + g)
-        s_ref[b] = e
-        return jnp.where(lane64 == b, jnp.sum(e, axis=1, keepdims=True), acc)
-
-    row = lax.fori_loop(0, 64, first_rows, jnp.ones((64, 128), jnp.float32))
+        f = column(f1, b)
+        t = None
+        for k in range(KP):
+            e = jnp.exp(s_ref[b, :, ks(k)] + f + tm_ref[rows_at(k, b), :])
+            s_ref[b, :, ks(k)] = e
+            t = e if t is None else t + e
+        return jnp.where(lane64 == home(b), jnp.sum(t, axis=1, keepdims=True), acc)
+
+    row = blocks(first_rows, jnp.ones((64, 128), jnp.float32))
     u = amass / row_exchange(1, row, None, total)
 
     def cols(u):
         def body(b, carry):
-            t = jnp.sum(s_ref[b] * column(u, b), axis=0, keepdims=True)
+            c = column(u, b)
             for k in range(KP):
-                ts_ref[rows_at(k, b), :] = t[:, k * 128 : k * 128 + 128]
+                ts_ref[rows_at(k, b), :] = jnp.sum(s_ref[b, :, ks(k)] * c, axis=0, keepdims=True)
             return carry
 
-        lax.fori_loop(0, 64, body, 0)
+        blocks(body, 0)
         return compact(collect(ts_ref[...]))
 
     v = bmass / col_exchange(1, cols(u), None, total)[0]
@@ -394,12 +481,15 @@
     tm_ref[...] = spread_out(expand(v))
 
     def rows(b, acc):
-        g = jnp.concatenate([tm_ref[rows_at(k, b), :] for k in range(KP)], axis=1)
-        return jnp.where(lane64 == b, jnp.sum(s_ref[b] * g, axis=1, keepdims=True), acc)
-
-    row = lax.fori_loop(0, 64, rows, jnp.ones((64, 128), jnp.float32))
+        t = functools.reduce(
+            jnp.add, [s_ref[b, :, ks(k)] * tm_ref[rows_at(k, b), :] for k in range(KP)]
+        )
+        return jnp.where(lane64 == home(b), jnp.sum(t, axis=1, keepdims=True), acc)
+
+    row = blocks(rows, jnp.ones((64, 128), jnp.float32))
     u = amass / row_exchange(2, row, None, total)
-    fout_ref[...] = f1 + jnp.log(u)
+    f = f1 + jnp.log(u)
+    fout_ref[...] = jnp.concatenate([f, pltpu.roll(f, 96, 1)], axis=0).T[0:32]
     v = bmass / col_exchange(2, cols(u), None, total)[0]
     gout_ref[...] = g1 + jnp.log(v)
 
@@ -410,35 +500,26 @@
 def body(residuals, codebook, item_weight, code_capacity, pairs):
     items = residuals.shape[1]
     codes = codebook.shape[1]
-    nb = items // BLOCK
-    live = pairs >= 0
-    slot = jnp.arange(pairs.shape[1], dtype=jnp.int32)
-    rank = jnp.sum(live[:, None, :] & (slot[None, None, :] < slot[None, :, None]), axis=2)
-    pick = live[:, None, :] & (rank[:, None, :] == jnp.arange(SLOTS, dtype=jnp.int32)[None, :, None])
-    tgt = jnp.sum(jnp.where(pick, pairs[:, None, :] + 1, 0), axis=2) - 1
-    flip = jnp.arange(SLOTS, dtype=jnp.int32) & 1
-    ids = jnp.bitwise_xor(jnp.maximum(tgt, 0), flip[None, :])
-    by_pair = tgt.T.reshape(KP, 2, nb)
-    tgtt = by_pair.transpose(1, 0, 2).reshape(2, 1, KP * nb)
-    tgtrow = jnp.repeat(by_pair.transpose(0, 2, 1).reshape(KP * nb, 2), 64, axis=1)
-    wt = jnp.pad(item_weight.reshape(nb, BLOCK).T, ((0, 0), (0, 128 - nb)), constant_values=1.0)
-    cap = code_capacity.reshape(2, 64, BLOCK).transpose(1, 0, 2).reshape(64, 128)
     vm = pl.BlockSpec(memory_space=pltpu.VMEM)
     hbm = pl.BlockSpec(memory_space=pl.ANY)
     f32, bf16 = jnp.float32, jnp.bfloat16
     dma = pltpu.SemaphoreType.DMA
     f, g = pl.pallas_call(
         kernel,
-        out_shape=[jax.ShapeDtypeStruct((64, 128), f32), jax.ShapeDtypeStruct((64, 128), f32)],
-        in_specs=[hbm, hbm, vm, vm, vm, vm, pl.BlockSpec(memory_space=pltpu.SMEM)],
+        out_shape=[jax.ShapeDtypeStruct((32, 128), f32), jax.ShapeDtypeStruct((64, 128), f32)],
+        in_specs=[hbm, hbm, vm, vm, vm],
         out_specs=[vm, vm],
         scratch_shapes=[
             pltpu.VMEM((16, 2, 8, codes), f32),
             pltpu.VMEM((8, 32, items), f32),
-            pltpu.VMEM((128, 256, 128), bf16),
-            pltpu.VMEM((128, 256, 128), bf16),
+            pltpu.VMEM((128, 16, 16, 128), bf16),
+            pltpu.VMEM((128, 16, 16, 128), bf16),
             pltpu.VMEM((64, 128, 256), bf16),
             pltpu.VMEM((64, 64, 512), f32),
+            pltpu.VMEM((64, 128), jnp.int32),
+            pltpu.VMEM((256, 128), jnp.int32),
+            pltpu.VMEM((64, 128), jnp.int32),
+            pltpu.SMEM((64, 128), jnp.int32),
             pltpu.VMEM((256, 128), f32),
             pltpu.VMEM((256, 128), f32),
             pltpu.VMEM((3, 8, 40, 128), f32),
@@ -448,7 +529,7 @@
             dma((40,)),
             dma((8,)),
             dma((8,)),
-            dma((3,)),
+            dma((4,)),
             dma((21,)),
             dma((21,)),
             dma((9,)),
@@ -459,10 +540,14 @@
         compiler_params=pltpu.CompilerParams(
             collective_id=0, has_side_effects=True, vmem_limit_bytes=60 * 1024 * 1024
         ),
-    )(codebook.reshape(2, 8, codes), residuals, wt, cap, tgtrow, tgtt, ids)
-    f = f[:, :nb].T.reshape(items)
-    g = g.reshape(64, 2, BLOCK).transpose(1, 0, 2).reshape(codes)
-    return f, g
+    )(
+        codebook.reshape(2, 8, codes),
+        residuals,
+        item_weight.reshape(32, 128),
+        code_capacity.reshape(64, 128),
+        pairs,
+    )
+    return f.reshape(items), g.reshape(codes)
 
 
 def solution(mesh):

time: 178 us -> 136 us (0.76)
  Pallas kernels: 169 us -> 132 us
  local copies, waits for them, and re-layouts: 6.24 us -> 3.35 us
    pallas_call x1, Pallas kernels: 169 us -> 132 us  [body(): pl.pallas_call(kernel, out_shape=[jax.ShapeDtypeStruct((32, 128), f32), j...]
    reshape x11 -> x0, local copies, waits for them, and re-layouts: 4.66 us -> none  [the longest x3 1.55 us: body(): g = g.reshape(64, 2, BLOCK).transpose(1, 0, 2).reshape(codes)]
    unnamed x8 -> x5, local copies, waits for them, and re-layouts: 0.64 us -> 3.35 us
where the time goes in v2:
time: 136 us
  Pallas kernels  132 us (97%)
  local copies, waits for them, and re-layouts  3.35 us (2%)
    pallas_call x1, Pallas kernels, body(): pl.pallas_call(kernel, out_shape=[jax.ShapeDtypeStruct((32, 128), f32), j...  132 us
    unnamed x5, local copies, waits for them, and re-layouts  3.35 us

profile of v2, /device:TPU:0, one launch (start us, length us, event | category | flops | bytes accessed | tf_op | source)
XLA Modules:
  0.0 135.6 jit_solution(4322195331871904139)
XLA Ops:
  0.6 1.4 %copy.7.pairs_ref = s32[64,16]{1,0:T(8,128)} copy(s32[64,16]{0,1:T(8,128)} %param.9) | data formatting | bytes 8192 | tf_op args[4]
  2.0 131.6 %shard_map.68 = (f32[32,128]{1,0:T(8,128)}, f32[64,128]{1,0:T(8,128)}) custom-call(f32[2,8,8192]{2,1,0:T(8,128)} %bitcast.5, f32[32,4096]{1,0:T(8,128)} %res_ref.1, f32[32,128]{1,0:T(8,128)} %bitcast.8, f32[64,128]{1,0:T(8,128)} %bitcast.6, s32[64,16]{1,0:T(8,128)} %copy.7.pairs_ref), custom_call_target="tpu_custom_call" | custom-call | tf_op jit(solution)/shard_map/pallas_call | solution.py:507
  133.6 0.0 copy-start
  133.6 1.3 copy.10
  134.9 0.0 copy-done
  134.9 0.6 copy.11
Async XLA Ops:
  133.6 1.3 copy-start

commit v3 on v2

--- a/solution.py
+++ b/solution.py
@@ -275,7 +275,8 @@
         halves(k)
     work(len(tasks))
 
-    UN = 4
+    UN = 8
+    leftw = lax.broadcasted_iota(jnp.int32, (width, 128), 1) < 64
 
     def rows_at(k, b):
         return pl.ds(k * 64 + b, 1)
@@ -299,25 +300,29 @@
 
     def score_block(b, acc):
         a = rt[b]
-        ss = []
+        wh, wl = [], []
         for k in range(KP):
             i0 = ids_ref[b, 2 * k]
             i1 = ids_ref[b, 2 * k + 1]
-            wh = jnp.concatenate([vh[i0].reshape(width, 128), vh[i1].reshape(width, 128)], axis=1)
-            wl = jnp.concatenate([vl[i0].reshape(width, 128), vl[i1].reshape(width, 128)], axis=1)
-            d1 = jnp.dot(a, wh, preferred_element_type=jnp.float32)
-            d2 = jnp.dot(a[0:64], wl, preferred_element_type=jnp.float32)
+            wh.append(jnp.where(leftw, vh[i0].reshape(width, 128), vh[i1].reshape(width, 128)))
+            wl.append(jnp.where(leftw, vl[i0].reshape(width, 128), vl[i1].reshape(width, 128)))
+        ss = []
+        for k in range(0, KP, 2):
+            d1 = jnp.dot(a, jnp.concatenate(wh[k : k + 2], axis=1), preferred_element_type=jnp.float32)
+            d2 = jnp.dot(
+                a[0:64], jnp.concatenate(wl[k : k + 2], axis=1), preferred_element_type=jnp.float32
+            )
             t = d1[0:64] + (d1[64:128] + d2)
-            s = jnp.where(left, t[:, 0:128], t[:, 128:256])
-            s = jnp.where(tgt_ref[rows_at(k, b), :] >= 0, s, NEG)
-            s_ref[b, :, ks(k)] = s
-            ss.append(s)
+            ss += [t[:, 0:128], t[:, 128:256]]
+        for k in range(KP):
+            ss[k] = jnp.where(tgt_ref[rows_at(k, b), :] >= 0, ss[k], NEG)
+            s_ref[b, :, ks(k)] = ss[k]
         m = jnp.max(functools.reduce(jnp.maximum, ss), axis=1, keepdims=True)
         t = functools.reduce(jnp.add, [jnp.exp(s - m) for s in ss])
         t = jnp.sum(t, axis=1, keepdims=True)
         return jnp.where(lane64 == home(b), m + jnp.log(t), acc)
 
-    row = blocks(score_block, jnp.zeros((64, 128), jnp.float32), 2)
+    row = blocks(score_block, jnp.zeros((64, 128), jnp.float32), 8)
 
     lane32 = lax.broadcasted_iota(jnp.int32, (32, 128), 1) < 64
 

time: 136 us -> 122 us (0.90)
  Pallas kernels: 132 us -> 117 us
    pallas_call x1, Pallas kernels: 132 us -> 117 us  [body(): pl.pallas_call(kernel, out_shape=[jax.ShapeDtypeStruct((32, 128), f32), j...]
where the time goes in v3:
time: 122 us; the launch traced here: 121 us
  Pallas kernels  117 us (96%)
  local copies, waits for them, and re-layouts  3.35 us (3%)
    pallas_call x1, Pallas kernels, body(): pl.pallas_call(kernel, out_shape=[jax.ShapeDtypeStruct((32, 128), f32), j...  117 us
    unnamed x5, local copies, waits for them, and re-layouts  3.35 us

profile of v3, /device:TPU:0, one launch (start us, length us, event | category | flops | bytes accessed | tf_op | source)
XLA Modules:
  0.0 121.4 jit_solution(11285312006120003417)
XLA Ops:
  0.6 1.4 %copy.7.pairs_ref = s32[64,16]{1,0:T(8,128)} copy(s32[64,16]{0,1:T(8,128)} %param.9) | data formatting | bytes 8192 | tf_op args[4]
  2.0 117.4 %shard_map.68 = (f32[32,128]{1,0:T(8,128)}, f32[64,128]{1,0:T(8,128)}) custom-call(f32[2,8,8192]{2,1,0:T(8,128)} %bitcast.5, f32[32,4096]{1,0:T(8,128)} %res_ref.1, f32[32,128]{1,0:T(8,128)} %bitcast.8, f32[64,128]{1,0:T(8,128)} %bitcast.6, s32[64,16]{1,0:T(8,128)} %copy.7.pairs_ref), custom_call_target="tpu_custom_call" | custom-call | tf_op jit(solution)/shard_map/pallas_call | solution.py:512
  119.5 0.0 copy-start
  119.5 1.3 %copy.10 = f32[4096]{0:T(1024)} copy(f32[4096]{0:T(1024)} %bitcast.9) | data formatting | bytes 32768
  120.8 0.0 copy-done
  120.8 0.6 copy.11
Async XLA Ops:
  119.5 1.3 %copy-start = (f32[64,128]{1,0:T(8,128)S(1)}, f32[64,128]{1,0:T(8,128)}, u32[]{:S(2)}) copy-start(f32[64,128]{1,0:T(8,128)} %get-tuple-element.5) | copy-start | bytes 98308

commit v4 on v3

--- a/solution.py
+++ b/solution.py
@@ -12,6 +12,7 @@
 SLOTS = 8
 KP = SLOTS // 2
 NEG = -1e30
+ORDER = [(0, 0), (0, 3), (3, 0), (0, 1), (1, 0), (0, 2), (2, 0), (3, 3), (1, 3), (3, 1), (1, 1), (3, 2), (2, 3), (1, 2), (2, 1), (2, 2)]
 SOFTNESS = 0.1
 MESH = pl.DeviceIdType.MESH
 
@@ -99,7 +100,6 @@
     pl.semaphore_wait(bar, 13)
 
     half = cd // 2
-    LO, HI = slice(0, half), slice(half, cd)
     sends = []
 
     def put(src, dst, ss, rs, dev):
@@ -121,29 +121,30 @@
     pos = [(y, z), (z, y)]
     cnt = [0]
 
-    def piece(h, p, s, cols=None, own=False):
-        if own:
-            return cb_ref.at[h]
-        d = place(h, p, s)
-        if cols is None:
-            return cg.at[d, h]
-        return cg.at[d, h, :, pl.ds(cols.start, cols.stop - cols.start)]
-
-    def cput(h, src_ps, cols, to, own=False):
+    def cput(h, src_ps, c, to, own=False):
         i = cnt[0]
         cnt[0] += 1
-        src = piece(h, *src_ps, cols, own)
-        dst = piece(h, *src_ps, cols)
+        col = pl.ds(c * half, half)
+        dst = cg.at[place(h, *src_ps), h, :, col]
+        src = cb_ref.at[h, :, col] if own else dst
         return put(src, dst, csend.at[i], crecv.at[i], where_to(h, *to))
 
+    def first(d):
+        return 0 if d > 0 else 1
+
+    dirs = [(h, d) for d in (1, -1) for h in range(2)]
     prim, sec = {}, {}
     locals_ = []
+    for turn in range(2):
+        for h, d in dirs:
+            p, s = pos[h]
+            c = first(d) ^ turn
+            prim[h, d, c] = cput(h, (p, s), c, (p + d, s), True)
+        for h, d in dirs:
+            p, s = pos[h]
+            c = first(d) ^ turn
+            sec[h, 0, d, c] = cput(h, (p, s), c, (p, s + d), True)
     for h in range(2):
-        p, s = pos[h]
-        prim[h, 1] = cput(h, (p, s), None, (p + 1, s), True)
-        prim[h, -1] = cput(h, (p, s), None, (p - 1, s), True)
-        sec[h, 0, 1] = cput(h, (p, s), None, (p, s + 1), True)
-        sec[h, 0, -1] = cput(h, (p, s), None, (p, s - 1), True)
         lc = pltpu.make_async_copy(cb_ref.at[h], cg.at[item, h], lsem.at[h])
         lc.start()
         locals_.append(lc)
@@ -159,9 +160,9 @@
         rcnt[0] += 1
         d = rdev(xx)
         if cols is None:
-            dst = rg.at[d]
+            dst = rg.at[pl.ds(2 * d, 2)]
         else:
-            dst = rg.at[d, :, pl.ds(cols * rhalf, rhalf)]
+            dst = rg.at[pl.ds(2 * d, 2), :, pl.ds(cols * rhalf, rhalf)]
         return put(res_ref if own else dst, dst, rsend.at[i], rrecv.at[i], ac(to))
 
     other = x * 2 + (1 - core)
@@ -169,114 +170,12 @@
     rp[1] = rput(x, None, rdev(x + 1), True)
     rp[-1] = rput(x, None, rdev(x - 1), True)
     rc = [rput(x, None, other, True)]
-    lc = pltpu.make_async_copy(res_ref, rg.at[code], lsem.at[2])
+    lc = pltpu.make_async_copy(res_ref, rg.at[pl.ds(2 * code, 2)], lsem.at[2])
     lc.start()
     locals_.append(lc)
 
-    tasks = []
-    parts = {}
-
-    def split_items(c, carry):
-        col = pl.ds(pl.multiple_of(c * 128, 128), 128)
-        v = rg[:, :, col].reshape(width, 128).T * scale
-        hi = v.astype(jnp.bfloat16)
-        lo = (v - hi.astype(jnp.float32)).astype(jnp.bfloat16)
-        for b in range(2):
-            rt[2 * c + b, 0:64, :] = hi[b * 64 : b * 64 + 64]
-            rt[2 * c + b, 64:128, :] = lo[b * 64 : b * 64 + 64]
-        return carry
-
-    def split_codes(d):
-        def step(j, carry):
-            for r in range(8):
-                q = j * 8 + r
-                col = pl.ds(pl.multiple_of(q * 128, 128), 128)
-                v = cg[d, :, :, col].reshape(16, 128)
-                for b, t in ((0, v), (1, pltpu.roll(v, 64, 1))):
-                    hi = t.astype(jnp.bfloat16)
-                    vh[2 * q + b, d] = hi
-                    vl[2 * q + b, d] = (t - hi.astype(jnp.float32)).astype(jnp.bfloat16)
-            return carry
-
-        lax.fori_loop(0, cd // 1024, step, 0)
-
-    def got(h, op, os, share):
-        dy, dz = ((op, os) if h == 0 else (os, op))
-        key = dy % 4, dz % 4
-        parts[key] = parts.get(key, 0) + share
-        if parts[key] == 4:
-            d = ((z + dz) % 4) * 4 + (y + dy) % 4
-            tasks.append(lambda: split_codes(d))
-
-    def work(n):
-        for _ in range(min(n, len(tasks))):
-            tasks.pop(0)()
-
-    ph, sh = {}, {}
-    for d in (1, -1):
-        for h in range(2):
-            p, s = pos[h]
-            prim[h, d].wait_recv()
-            got(h, -d, 0, 2)
-            ph[h, d] = cput(h, (p - d, s), LO if d > 0 else HI, (p + d, s))
-            sec[h, d, 1] = cput(h, (p - d, s), None, (p, s + 1))
-            sec[h, d, -1] = cput(h, (p - d, s), None, (p, s - 1))
-        rp[d].wait_recv()
-        rp[2 * d] = rput(x - d, 0 if d > 0 else 1, rdev(x + d))
-        rc.append(rput(x - d, None, other))
-        for h in range(2):
-            p, s = pos[h]
-            sec[h, 0, d].wait_recv()
-            got(h, 0, -d, 2)
-            sh[h, 0, d] = cput(h, (p, s - d), LO if d > 0 else HI, (p, s + d))
-    for c in locals_:
-        c.wait()
-    for h in range(2):
-        got(h, 0, 0, 2)
-    for h in range(2):
-        p, s = pos[h]
-        work(1)
-        ph[h, 1].wait_recv()
-        ph[h, -1].wait_recv()
-        got(h, 2, 0, 2)
-        sec[h, 2, 1] = cput(h, (p + 2, s), None, (p, s + 1))
-        sec[h, 2, -1] = cput(h, (p + 2, s), None, (p, s - 1))
-    rp[2].wait_recv()
-    rp[-2].wait_recv()
-    rc.append(rput(x + 2, None, other))
-    offs = {0: 0, 1: -1, -1: 1, 2: 2}
-
-    def secondary(k):
-        for d in (1, -1):
-            for h in range(2):
-                p, s = pos[h]
-                work(1)
-                sec[h, k, d].wait_recv()
-                got(h, offs[k], -d, 2)
-                sh[h, k, d] = cput(h, (p + offs[k], s - d), LO if d > 0 else HI, (p, s + d))
-
-    def halves(k):
-        for d in (1, -1):
-            for h in range(2):
-                work(1)
-                sh[h, k, d].wait_recv()
-                got(h, offs[k], 2, 1)
-
-    secondary(1)
-    for c in rc:
-        c.wait_recv()
-    for g in range(8):
-        n = idv // 128 // 8
-        tasks.append(lambda g=g, n=n: lax.fori_loop(g * n, g * n + n, split_items, 0))
-    secondary(-1)
-    halves(0)
-    secondary(2)
-    for k in (1, -1, 2):
-        halves(k)
-    work(len(tasks))
-
     UN = 8
-    leftw = lax.broadcasted_iota(jnp.int32, (width, 128), 1) < 64
+    leftw = lax.broadcasted_iota(jnp.int32, (width // 2, 128), 1) < 64
 
     def rows_at(k, b):
         return pl.ds(k * 64 + b, 1)
@@ -298,14 +197,17 @@
 
         return lax.fori_loop(0, 64 // un, step, init)
 
-    def score_block(b, acc):
-        a = rt[b]
+    def score_part(b, part):
+        r8 = pl.ds(part * 8, 8)
         wh, wl = [], []
         for k in range(KP):
             i0 = ids_ref[b, 2 * k]
             i1 = ids_ref[b, 2 * k + 1]
-            wh.append(jnp.where(leftw, vh[i0].reshape(width, 128), vh[i1].reshape(width, 128)))
-            wl.append(jnp.where(leftw, vl[i0].reshape(width, 128), vl[i1].reshape(width, 128)))
+            for ref, out in ((vh, wh), (vl, wl)):
+                one = ref[i0, r8].reshape(width // 2, 128)
+                two = ref[i1, r8].reshape(width // 2, 128)
+                out.append(jnp.where(leftw, one, two))
+        a = rt[b, :, part * 128 : part * 128 + 128]
         ss = []
         for k in range(0, KP, 2):
             d1 = jnp.dot(a, jnp.concatenate(wh[k : k + 2], axis=1), preferred_element_type=jnp.float32)
@@ -314,8 +216,139 @@
             )
             t = d1[0:64] + (d1[64:128] + d2)
             ss += [t[:, 0:128], t[:, 128:256]]
+        return ss
+
+    def score_half(g):
+        for r in range(8):
+            b = g * 8 + r
+            for k, t in enumerate(score_part(b, 0)):
+                s_ref[b, :, ks(k)] = t
+
+    tasks = []
+    parts = {}
+    ready = [0]
+
+    def split_items(c, carry):
+        col = pl.ds(pl.multiple_of(c * 128, 128), 128)
+        v = jnp.concatenate([rg[source(k), :, col] for k in ORDER], axis=0).T * scale
+        hi = v.astype(jnp.bfloat16)
+        lo = (v - hi.astype(jnp.float32)).astype(jnp.bfloat16)
+        for b in range(2):
+            rt[2 * c + b, 0:64, :] = hi[b * 64 : b * 64 + 64]
+            rt[2 * c + b, 64:128, :] = lo[b * 64 : b * 64 + 64]
+        return carry
+
+    def source(key):
+        return ((z + key[1]) % 4) * 4 + (y + key[0]) % 4
+
+    def split_codes(d, rank):
+        def step(j, carry):
+            for r in range(8):
+                q = j * 8 + r
+                col = pl.ds(pl.multiple_of(q * 128, 128), 128)
+                v = cg[d, :, :, col].reshape(16, 128)
+                for b, t in ((0, v), (1, pltpu.roll(v, 64, 1))):
+                    hi = t.astype(jnp.bfloat16)
+                    vh[2 * q + b, rank] = hi
+                    vl[2 * q + b, rank] = (t - hi.astype(jnp.float32)).astype(jnp.bfloat16)
+            return carry
+
+        lax.fori_loop(0, cd // 1024, step, 0)
+
+    def got(h, op, os, share):
+        dy, dz = ((op, os) if h == 0 else (os, op))
+        key = dy % 4, dz % 4
+        parts[key] = parts.get(key, 0) + share
+        if parts[key] == 4:
+            r = ready[0]
+            ready[0] += 1
+            assert ORDER[r] == key
+            tasks.append(lambda: split_codes(source(key), r))
+            if r == 7:
+                for g in range(8):
+                    tasks.append(lambda g=g: score_half(g))
+
+    def work(n):
+        for _ in range(min(n, len(tasks))):
+            tasks.pop(0)()
+
+    ph, sh = {}, {}
+    offs = {0: 0, 1: -1, -1: 1, 2: 2}
+
+    def pass_on(h, k, c):
+        p, s = pos[h]
+        for d in (1, -1) if c == 0 else (-1, 1):
+            sec[h, k, d, c] = cput(h, (p + offs[k], s), c, (p, s + d))
+
+    def forward(k):
+        for h, d in dirs:
+            p, s = pos[h]
+            c = first(d)
+            if k:
+                work(1)
+            sec[h, k, d, c].wait_recv()
+            sh[h, k, d] = cput(h, (p + offs[k], s - d), c, (p, s + d))
+            got(h, offs[k], -d, 1)
+
+    def take(k, turn):
+        for h, d in dirs:
+            work(1)
+            if turn:
+                sec[h, k, d, 1 - first(d)].wait_recv()
+                got(h, offs[k], -d, 1)
+            else:
+                sh[h, k, d].wait_recv()
+                got(h, offs[k], 2, 1)
+
+    for h, d in dirs:
+        p, s = pos[h]
+        c = first(d)
+        prim[h, d, c].wait_recv()
+        ph[h, d] = cput(h, (p - d, s), c, (p + d, s))
+        pass_on(h, d, c)
+        got(h, -d, 0, 1)
+    forward(0)
+    for h, d in dirs:
+        c = 1 - first(d)
+        prim[h, d, c].wait_recv()
+        pass_on(h, d, c)
+        got(h, -d, 0, 1)
+    for d in (1, -1):
+        rp[d].wait_recv()
+        rp[2 * d] = rput(x - d, 0 if d > 0 else 1, rdev(x + d))
+        rc.append(rput(x - d, None, other))
+    for h, d in dirs:
+        ph[h, d].wait_recv()
+        pass_on(h, 2, first(d))
+        got(h, 2, 0, 1)
+    for c in locals_:
+        c.wait()
+    for h in range(2):
+        got(h, 0, 0, 2)
+    take(0, 1)
+    rp[2].wait_recv()
+    rp[-2].wait_recv()
+    rc.append(rput(x + 2, None, other))
+    forward(1)
+    forward(-1)
+    for c in rc:
+        c.wait_recv()
+    for g in range(8):
+        n = idv // 128 // 8
+        tasks.append(lambda g=g, n=n: lax.fori_loop(g * n, g * n + n, split_items, 0))
+    take(0, 0)
+    take(1, 1)
+    take(-1, 1)
+    forward(2)
+    take(2, 1)
+    for k in (1, -1, 2):
+        take(k, 0)
+    work(len(tasks))
+
+    def score_block(b, acc):
+        ss = score_part(b, 1)
         for k in range(KP):
-            ss[k] = jnp.where(tgt_ref[rows_at(k, b), :] >= 0, ss[k], NEG)
+            ss[k] = jnp.where(tgt_ref[rows_at(k, b), :] >= 0, ss[k] + s_ref[b, :, ks(k)], NEG)
             s_ref[b, :, ks(k)] = ss[k]
         m = jnp.max(functools.reduce(jnp.maximum, ss), axis=1, keepdims=True)
         t = functools.reduce(jnp.add, [jnp.exp(s - m) for s in ss])
@@ -516,7 +549,7 @@
         out_specs=[vm, vm],
         scratch_shapes=[
             pltpu.VMEM((16, 2, 8, codes), f32),
-            pltpu.VMEM((8, 32, items), f32),
+            pltpu.VMEM((16, 16, items), f32),
             pltpu.VMEM((128, 16, 16, 128), bf16),
             pltpu.VMEM((128, 16, 16, 128), bf16),
             pltpu.VMEM((64, 128, 256), bf16),
@@ -530,8 +563,8 @@
             pltpu.VMEM((3, 8, 40, 128), f32),
             pltpu.VMEM((3, 4, 72, 128), f32),
             pltpu.VMEM((3, 4, 72, 128), f32),
-            dma((40,)),
-            dma((40,)),
+            dma((64,)),
+            dma((64,)),
             dma((8,)),
             dma((8,)),
             dma((4,)),
@@ -547,7 +580,7 @@
         ),
     )(
         codebook.reshape(2, 8, codes),
-        residuals,
+        residuals.reshape(2, 16, items),
         item_weight.reshape(32, 128),
         code_capacity.reshape(64, 128),
         pairs,

time: 122 us -> 119 us (0.975)
  Pallas kernels: 117 us -> 115 us
    pallas_call x1, Pallas kernels: 117 us -> 115 us  [body(): pl.pallas_call(kernel, out_shape=[jax.ShapeDtypeStruct((32, 128), f32), j...]
where the time goes in v4:
time: 119 us
  Pallas kernels  115 us (97%)
  local copies, waits for them, and re-layouts  3.35 us (3%)
    pallas_call x1, Pallas kernels, body(): pl.pallas_call(kernel, out_shape=[jax.ShapeDtypeStruct((32, 128), f32), j...  115 us
    unnamed x5, local copies, waits for them, and re-layouts  3.35 us

profile of v4, /device:TPU:0, one launch (start us, length us, event | category | flops | bytes accessed | tf_op | source)
XLA Modules:
  0.0 119.2 jit_solution(7359205481727725761)
XLA Ops:
  0.6 1.4 %copy.7.pairs_ref = s32[64,16]{1,0:T(8,128)} copy(s32[64,16]{0,1:T(8,128)} %param.9) | data formatting | bytes 8192 | tf_op args[4]
  2.0 115.2 %shard_map.68 = (f32[32,128]{1,0:T(8,128)}, f32[64,128]{1,0:T(8,128)}) custom-call(f32[2,8,8192]{2,1,0:T(8,128)} %bitcast.6, f32[2,16,4096]{2,1,0:T(8,128)} %bitcast.7, f32[32,128]{1,0:T(8,128)} %bitcast.10, f32[64,128]{1,0:T(8,128)} %bitcast.8, s32[64,16]{1,0:T(8,128)} %copy.7.pairs_ref), custom_call_target="tpu_custom_call" | custom-call | tf_op jit(solution)/shard_map/pallas_call | solution.py:545
  117.2 0.0 copy-start
  117.2 1.3 %copy.10 = f32[4096]{0:T(1024)} copy(f32[4096]{0:T(1024)} %bitcast.11) | data formatting | bytes 32768
  118.6 0.0 copy-done
  118.6 0.6 copy.11
Async XLA Ops:
  117.2 1.3 %copy-start = (f32[64,128]{1,0:T(8,128)S(1)}, f32[64,128]{1,0:T(8,128)}, u32[]{:S(2)}) copy-start(f32[64,128]{1,0:T(8,128)} %get-tuple-element.5) | copy-start | bytes 98308

commit v5 on v4

--- a/solution.py
+++ b/solution.py
@@ -12,6 +12,8 @@
 SLOTS = 8
 KP = SLOTS // 2
 NEG = -1e30
+PARTS = 2
+LANES = 64 // PARTS
 ORDER = [(0, 0), (0, 3), (3, 0), (0, 1), (1, 0), (0, 2), (2, 0), (3, 3), (1, 3), (3, 1), (1, 1), (3, 2), (2, 3), (1, 2), (2, 1), (2, 2)]
 SOFTNESS = 0.1
 MESH = pl.DeviceIdType.MESH
@@ -31,6 +33,7 @@
     vl,
     rt,
     s_ref,
+    slots,
     padded,
     tgt_ref,
     ids_v,
@@ -77,9 +80,12 @@
     lane = lax.broadcasted_iota(jnp.int32, (1, 128), 1)
     left = lane < 64
     lane64 = lax.broadcasted_iota(jnp.int32, (64, 128), 1)
-    padded[...] = jnp.full((64, 128), -1, jnp.int32)
-    padded[:, 0:16] = pairs_ref[...]
-    named = padded[...]
+    sc = pltpu.make_async_copy(pairs_ref, slots, lsem.at[3])
+    sc.start()
+    padded[...] = jnp.full((128, 128), -1, jnp.int32)
+    sc.wait()
+    padded[0:16, 0:64] = slots[...]
+    named = padded[...].T[0:64]
     live = jnp.where(named >= 0, 1, 0)
     count = live
     for sh in (1, 2, 4, 8):
@@ -180,22 +186,22 @@
     def rows_at(k, b):
         return pl.ds(k * 64 + b, 1)
 
-    def home(b):
-        return (b & 1) * 32 + (b >> 1)
-
-    def column(f, b):
-        return jnp.sum(jnp.where(lane64 == home(b), f, 0.0), axis=1, keepdims=True)
+    def column(f, at):
+        return jnp.sum(jnp.where(lane64 == at, f, 0.0), axis=1, keepdims=True)
 
     def ks(k):
         return slice(k * 128, k * 128 + 128)
 
-    def blocks(body, init, un=UN):
+    def blocks(part, body, init, un=UN):
+        low = part * LANES
+
         def step(j, acc):
             for r in range(un):
-                acc = body(j * un + r, acc)
+                i = j * un + r
+                acc = body(2 * (low % 32 + i) + low // 32, low + i, acc)
             return acc
 
-        return lax.fori_loop(0, 64 // un, step, init)
+        return lax.fori_loop(0, LANES // un, step, init)
 
     def score_part(b, part):
         r8 = pl.ds(part * 8, 8)
@@ -345,7 +351,7 @@
         take(k, 0)
     work(len(tasks))
 
-    def score_block(b, acc):
+    def score_block(b, at, acc):
         ss = score_part(b, 1)
         for k in range(KP):
             ss[k] = jnp.where(tgt_ref[rows_at(k, b), :] >= 0, ss[k] + s_ref[b, :, ks(k)], NEG)
@@ -353,17 +359,28 @@
         m = jnp.max(functools.reduce(jnp.maximum, ss), axis=1, keepdims=True)
         t = functools.reduce(jnp.add, [jnp.exp(s - m) for s in ss])
         t = jnp.sum(t, axis=1, keepdims=True)
-        return jnp.where(lane64 == home(b), m + jnp.log(t), acc)
-
-    row = blocks(score_block, jnp.zeros((64, 128), jnp.float32), 8)
-
-    lane32 = lax.broadcasted_iota(jnp.int32, (32, 128), 1) < 64
-
-    def pack(r):
-        return jnp.where(lane32, r[0:32], pltpu.roll(r[32:64], 64, 1))
-
-    def unpack(m):
-        return jnp.concatenate([m, pltpu.roll(m, 64, 1)], axis=0)
+        return jnp.where(lane64 == at, m + jnp.log(t), acc)
+
+    def group(g):
+        return slice(g * LANES // 2, g * LANES // 2 + LANES // 2)
+
+    def pack(part, r):
+        out = r[group(0)] if part == 0 else pltpu.roll(r[group(0)], (-part * LANES) % 128, 1)
+        for g in range(1, 128 // LANES):
+            shift = ((g - part) * LANES) % 128
+            one = pltpu.roll(r[group(g)], shift, 1) if shift else r[group(g)]
+            out = jnp.where(lane < g * LANES, out, one)
+        return out
+
+    def unpack(part, m):
+        out = []
+        for g in range(128 // LANES):
+            shift = ((part - g) * LANES) % 128
+            out.append(pltpu.roll(m, shift, 1) if shift else m)
+        return jnp.concatenate(out, axis=0)
+
+    def of_part(part):
+        return (lane64 >= part * LANES) & (lane64 < part * LANES + LANES)
 
     def lse(parts):
         m = functools.reduce(jnp.maximum, parts)
@@ -373,56 +390,73 @@
     def total(parts):
         return functools.reduce(jnp.add, parts)
 
-    def row_exchange(n, r, extra, merge):
-        xrow[n, code, 0:32, :] = pack(r)
-        size = 32
+    def row_send(n, part, r, extra=None):
+        size = LANES // 2
+        xrow[n, part, code, 0:size, :] = pack(part, r)
         if extra is not None:
-            xrow[n, code, 32:40, :] = jnp.broadcast_to(extra, (8, 128))
-            size = 40
+            xrow[n, part, code, size : size + 8, :] = jnp.broadcast_to(extra, (8, 128))
+            size += 8
         cs = []
         for d in range(1, 8):
-            ref = xrow.at[n, code, pl.ds(0, size), :]
-            i = n * 7 + d - 1
+            ref = xrow.at[n, part, code, pl.ds(0, size), :]
+            i = (n * PARTS + part) * 7 + d - 1
             cs.append(put(ref, ref, rowsend.at[i], rowrecv.at[i], ac((code + d) % 8)))
+        return cs
+
+    def row_receive(n, part, cs, merge):
         for c in cs:
             c.wait_recv()
-        out = unpack(merge([xrow[n, q, 0:32, :] for q in range(8)]))
-        if extra is None:
-            return out
-        return out, total([xrow[n, q, 32:40, :] for q in range(8)])[0:1, 0:1]
-
-    def one_axis(n, buf, me, ssem, rsem, dev, val, extra, merge):
-        buf[n, me, 0:64, :] = val
-        size = 64
-        if extra is not None:
-            buf[n, me, 64:72, :] = jnp.broadcast_to(extra, (8, 128))
-            size = 72
-        cs = []
-        for d in range(1, 4):
-            ref = buf.at[n, me, pl.ds(0, size), :]
-            i = n * 3 + d - 1
-            cs.append(put(ref, ref, ssem.at[i], rsem.at[i], dev(d)))
-        for c in cs:
-            c.wait_recv()
-        out = merge([buf[n, q, 0:64, :] for q in range(4)])
-        if extra is None:
-            return out, None
-        return out, total([buf[n, q, 64:72, :] for q in range(4)])[0:1, 0:1]
+        return unpack(part, merge([xrow[n, part, q, 0 : LANES // 2, :] for q in range(8)]))
+
+    def rows_then_cols(n, row_body, extra, merge, finish, col_body):
+        sent = []
+        for part in range(PARTS):
+            r = blocks(part, row_body, jnp.ones((64, 128), jnp.float32))
+            sent.append(row_send(n, part, r, extra if part == 0 else None))
+        out = jnp.zeros((64, 128), jnp.float32)
+        for part in range(PARTS):
+            r = row_receive(n, part, sent[part], merge)
+            out = jnp.where(of_part(part), finish(r), out)
+            blocks(part, functools.partial(col_body, out), 0)
+        return out
 
     def col_exchange(n, val, extra, merge):
-        val, extra = one_axis(n, xy, y, ysend, yrecv, lambda d: at(z, y + d), val, extra, merge)
-        return one_axis(n, xz, z, zsend, zrecv, lambda d: at(z + d, y), val, extra, merge)
+        vals = [val[0:32], val[32:64]]
+        for stage in range(2):
+            cs = []
+            for axis, buf, me, ssem, rsem in ((0, xy, y, ysend, yrecv), (1, xz, z, zsend, zrecv)):
+                part = axis ^ stage
+                size = 32
+                buf[n, stage, me, 0:32, :] = vals[part]
+                if extra is not None and part == 0:
+                    buf[n, stage, me, 32:40, :] = jnp.broadcast_to(extra, (8, 128))
+                    size = 40
+                for d in (2, 1, 3):
+                    ref = buf.at[n, stage, me, pl.ds(0, size), :]
+                    i = (n * 2 + stage) * 3 + d - 1
+                    dev = at(z, y + d) if axis == 0 else at(z + d, y)
+                    cs.append(put(ref, ref, ssem.at[i], rsem.at[i], dev))
+            for c in cs:
+                c.wait_recv()
+            merged = [None, None]
+            for axis, buf in ((0, xy), (1, xz)):
+                part = axis ^ stage
+                merged[part] = merge([buf[n, stage, q, 0:32, :] for q in range(4)])
+                if extra is not None and part == 0:
+                    more = total([buf[n, stage, q, 32:40, :] for q in range(4)])[0:1, 0:1]
+            vals = merged
+            extra = more if extra is not None else None
+        return jnp.concatenate(vals, axis=0), extra
 
     turned = jnp.concatenate([wt_ref[...], jnp.ones((96, 128), jnp.float32)], axis=0).T
     wt = jnp.where(lane64 < 32, turned[0:64], pltpu.roll(turned[64:128], 32, 1))
     cap = cap_ref[...]
     wsum = jnp.sum(jnp.where(lane64 < 64, wt, 0.0), keepdims=True)
     csum = jnp.sum(cap, keepdims=True)
-    row, capacity = row_exchange(0, row, csum, lse)
-    f1 = jnp.log(wt) - row
-
-    def col_first(b, carry):
-        f = column(f1, b)
+    logwt = jnp.log(wt)
+
+    def col_first(f1, b, at, carry):
+        f = column(f1, at)
         for k in range(KP):
             c = s_ref[b, :, ks(k)] + f
             m = jnp.max(c, axis=0, keepdims=True)
@@ -430,7 +464,9 @@
             ts_ref[rows_at(k, b), :] = jnp.sum(jnp.exp(c - m), axis=0, keepdims=True)
         return carry
 
-    blocks(col_first, 0)
+    f1 = rows_then_cols(0, score_block, csum, lse, lambda r: logwt - r, col_first)
+    extra = slice(LANES // 2, LANES // 2 + 8)
+    capacity = total([xrow[0, 0, q, extra, :] for q in range(8)])[0:1, 0:1]
 
     block = lax.broadcasted_iota(jnp.int32, (128, 128), 0)
 
@@ -492,43 +528,36 @@
 
     tm_ref[...] = spread_out(expand(g1))
 
-    def first_rows(b, acc):
-        f = column(f1, b)
+    def first_rows(b, at, acc):
+        f = column(f1, at)
         t = None
         for k in range(KP):
             e = jnp.exp(s_ref[b, :, ks(k)] + f + tm_ref[rows_at(k, b), :])
             s_ref[b, :, ks(k)] = e
             t = e if t is None else t + e
-        return jnp.where(lane64 == home(b), jnp.sum(t, axis=1, keepdims=True), acc)
-
-    row = blocks(first_rows, jnp.ones((64, 128), jnp.float32))
-    u = amass / row_exchange(1, row, None, total)
-
-    def cols(u):
-        def body(b, carry):
-            c = column(u, b)
-            for k in range(KP):
-                ts_ref[rows_at(k, b), :] = jnp.sum(s_ref[b, :, ks(k)] * c, axis=0, keepdims=True)
-            return carry
-
-        blocks(body, 0)
-        return compact(collect(ts_ref[...]))
-
-    v = bmass / col_exchange(1, cols(u), None, total)[0]
+        return jnp.where(lane64 == at, jnp.sum(t, axis=1, keepdims=True), acc)
+
+    def cols(u, b, at, carry):
+        c = column(u, at)
+        for k in range(KP):
+            ts_ref[rows_at(k, b), :] = jnp.sum(s_ref[b, :, ks(k)] * c, axis=0, keepdims=True)
+        return carry
+
+    u = rows_then_cols(1, first_rows, None, total, lambda r: amass / r, cols)
+    v = bmass / col_exchange(1, compact(collect(ts_ref[...])), None, total)[0]
 
     tm_ref[...] = spread_out(expand(v))
 
-    def rows(b, acc):
+    def rows(b, at, acc):
         t = functools.reduce(
             jnp.add, [s_ref[b, :, ks(k)] * tm_ref[rows_at(k, b), :] for k in range(KP)]
         )
-        return jnp.where(lane64 == home(b), jnp.sum(t, axis=1, keepdims=True), acc)
-
-    row = blocks(rows, jnp.ones((64, 128), jnp.float32))
-    u = amass / row_exchange(2, row, None, total)
+        return jnp.where(lane64 == at, jnp.sum(t, axis=1, keepdims=True), acc)
+
+    u = rows_then_cols(2, rows, None, total, lambda r: amass / r, cols)
     f = f1 + jnp.log(u)
     fout_ref[...] = jnp.concatenate([f, pltpu.roll(f, 96, 1)], axis=0).T[0:32]
-    v = bmass / col_exchange(2, cols(u), None, total)[0]
+    v = bmass / col_exchange(2, compact(collect(ts_ref[...])), None, total)[0]
     gout_ref[...] = g1 + jnp.log(v)
 
     for c in sends:
@@ -545,7 +574,7 @@
     f, g = pl.pallas_call(
         kernel,
         out_shape=[jax.ShapeDtypeStruct((32, 128), f32), jax.ShapeDtypeStruct((64, 128), f32)],
-        in_specs=[hbm, hbm, vm, vm, vm],
+        in_specs=[hbm, hbm, vm, vm, hbm],
         out_specs=[vm, vm],
         scratch_shapes=[
             pltpu.VMEM((16, 2, 8, codes), f32),
@@ -554,26 +583,27 @@
             pltpu.VMEM((128, 16, 16, 128), bf16),
             pltpu.VMEM((64, 128, 256), bf16),
             pltpu.VMEM((64, 64, 512), f32),
-            pltpu.VMEM((64, 128), jnp.int32),
+            pltpu.VMEM((16, 64), jnp.int32),
+            pltpu.VMEM((128, 128), jnp.int32),
             pltpu.VMEM((256, 128), jnp.int32),
             pltpu.VMEM((64, 128), jnp.int32),
             pltpu.SMEM((64, 128), jnp.int32),
             pltpu.VMEM((256, 128), f32),
             pltpu.VMEM((256, 128), f32),
-            pltpu.VMEM((3, 8, 40, 128), f32),
-            pltpu.VMEM((3, 4, 72, 128), f32),
-            pltpu.VMEM((3, 4, 72, 128), f32),
+            pltpu.VMEM((3, PARTS, 8, LANES // 2 + 8, 128), f32),
+            pltpu.VMEM((3, 2, 4, 40, 128), f32),
+            pltpu.VMEM((3, 2, 4, 40, 128), f32),
             dma((64,)),
             dma((64,)),
             dma((8,)),
             dma((8,)),
             dma((4,)),
-            dma((21,)),
-            dma((21,)),
-            dma((9,)),
-            dma((9,)),
-            dma((9,)),
-            dma((9,)),
+            dma((21 * PARTS,)),
+            dma((21 * PARTS,)),
+            dma((18,)),
+            dma((18,)),
+            dma((18,)),
+            dma((18,)),
         ],
         compiler_params=pltpu.CompilerParams(
             collective_id=0, has_side_effects=True, vmem_limit_bytes=60 * 1024 * 1024
@@ -583,7 +613,7 @@
         residuals.reshape(2, 16, items),
         item_weight.reshape(32, 128),
         code_capacity.reshape(64, 128),
-        pairs,
+        pairs.T,
     )
     return f.reshape(items), g.reshape(codes)
 

time: 119 us -> 113 us (0.950)
  Pallas kernels: 115 us -> 110 us
  local copies, waits for them, and re-layouts: 3.35 us -> 1.95 us
    pallas_call x1, Pallas kernels: 115 us -> 110 us  [body(): pl.pallas_call(kernel, out_shape=[jax.ShapeDtypeStruct((32, 128), f32), j...]
    unnamed x5 -> x4, local copies, waits for them, and re-layouts: 3.35 us -> 1.95 us
where the time goes in v5:
time: 113 us
  Pallas kernels  110 us (97%)
  local copies, waits for them, and re-layouts  1.95 us (2%)
    pallas_call x1, Pallas kernels, body(): pl.pallas_call(kernel, out_shape=[jax.ShapeDtypeStruct((32, 128), f32), j...  110 us

profile of v5, /device:TPU:0, one launch (start us, length us, event | category | flops | bytes accessed | tf_op | source)
XLA Modules:
  0.0 112.6 jit_solution(9416759087896987825)
XLA Ops:
  0.6 110.0 %shard_map.68 = (f32[32,128]{1,0:T(8,128)}, f32[64,128]{1,0:T(8,128)}) custom-call(f32[2,8,8192]{2,1,0:T(8,128)} %bitcast.7, f32[2,16,4096]{2,1,0:T(8,128)} %bitcast.8, f32[32,128]{1,0:T(8,128)} %bitcast.11, f32[64,128]{1,0:T(8,128)} %bitcast.9, s32[16,64]{1,0:T(8,128)} %bitcast.13), custom_call_target="tpu_custom_call" | custom-call | tf_op jit(solution)/shard_map/pallas_call | solution.py:574
  110.6 0.0 copy-start
  110.6 1.3 %copy.9 = f32[4096]{0:T(1024)} copy(f32[4096]{0:T(1024)} %bitcast.12) | data formatting | bytes 32768
  112.0 0.0 copy-done
  112.0 0.6 copy.10
Async XLA Ops:
  110.6 1.3 %copy-start = (f32[64,128]{1,0:T(8,128)S(1)}, f32[64,128]{1,0:T(8,128)}, u32[]{:S(2)}) copy-start(f32[64,128]{1,0:T(8,128)} %get-tuple-element.5) | copy-start | bytes 98308

commit v6 on v5

--- a/solution.py
+++ b/solution.py
@@ -12,7 +12,7 @@
 SLOTS = 8
 KP = SLOTS // 2
 NEG = -1e30
-PARTS = 2
+PARTS = 4
 LANES = 64 // PARTS
 ORDER = [(0, 0), (0, 3), (3, 0), (0, 1), (1, 0), (0, 2), (2, 0), (3, 3), (1, 3), (3, 1), (1, 1), (3, 2), (2, 3), (1, 2), (2, 1), (2, 2)]
 SOFTNESS = 0.1
@@ -233,6 +233,7 @@
     tasks = []
     parts = {}
     ready = [0]
+    per = [1]
 
     def split_items(c, carry):
         col = pl.ds(pl.multiple_of(c * 128, 128), 128)
@@ -290,7 +291,7 @@
         for h, d in dirs:
             p, s = pos[h]
             c = first(d)
-            if k:
+            if k in (1, -1):
                 work(1)
             sec[h, k, d, c].wait_recv()
             sh[h, k, d] = cput(h, (p + offs[k], s - d), c, (p, s + d))
@@ -298,7 +299,7 @@
 
     def take(k, turn):
         for h, d in dirs:
-            work(1)
+            work(per[0])
             if turn:
                 sec[h, k, d, 1 - first(d)].wait_recv()
                 got(h, offs[k], -d, 1)
@@ -346,6 +347,7 @@
     take(1, 1)
     take(-1, 1)
     forward(2)
+    per[0] = 2
     take(2, 1)
     for k in (1, -1, 2):
         take(k, 0)

time: 113 us -> 112 us (level)
  no operation moved by 1% of the time
where the time goes in v6:
time: 112 us
  Pallas kernels  109 us (97%)
  local copies, waits for them, and re-layouts  1.95 us (2%)
    pallas_call x1, Pallas kernels, body(): pl.pallas_call(kernel, out_shape=[jax.ShapeDtypeStruct((32, 128), f32), j...  109 us

profile of v6, /device:TPU:0, one launch (start us, length us, event | category | flops | bytes accessed | tf_op | source)
XLA Modules:
  0.0 111.9 jit_solution(485122456959985259)
XLA Ops:
  0.6 109.3 %shard_map.68 = (f32[32,128]{1,0:T(8,128)}, f32[64,128]{1,0:T(8,128)}) custom-call(f32[2,8,8192]{2,1,0:T(8,128)} %bitcast.7, f32[2,16,4096]{2,1,0:T(8,128)} %bitcast.8, f32[32,128]{1,0:T(8,128)} %bitcast.11, f32[64,128]{1,0:T(8,128)} %bitcast.9, s32[16,64]{1,0:T(8,128)} %bitcast.13), custom_call_target="tpu_custom_call" | custom-call | tf_op jit(solution)/shard_map/pallas_call | solution.py:576
  109.9 0.0 copy-start
  109.9 1.3 %copy.9 = f32[4096]{0:T(1024)} copy(f32[4096]{0:T(1024)} %bitcast.12) | data formatting | bytes 32768
  111.2 0.0 copy-done
  111.2 0.6 copy.10
Async XLA Ops:
  109.9 1.3 %copy-start = (f32[64,128]{1,0:T(8,128)S(1)}, f32[64,128]{1,0:T(8,128)}, u32[]{:S(2)}) copy-start(f32[64,128]{1,0:T(8,128)} %get-tuple-element.5) | copy-start | bytes 98308

commit v7 on v6

--- a/solution.py
+++ b/solution.py
@@ -399,7 +399,7 @@
             xrow[n, part, code, size : size + 8, :] = jnp.broadcast_to(extra, (8, 128))
             size += 8
         cs = []
-        for d in range(1, 8):
+        for d in (4, 3, 5, 2, 6, 1, 7):
             ref = xrow.at[n, part, code, pl.ds(0, size), :]
             i = (n * PARTS + part) * 7 + d - 1
             cs.append(put(ref, ref, rowsend.at[i], rowrecv.at[i], ac((code + d) % 8)))

time: 112 us -> 112 us (level)
  no operation moved by 1% of the time
where the time goes in v7:
time: 112 us
  Pallas kernels  109 us (97%)
  local copies, waits for them, and re-layouts  1.95 us (2%)
    pallas_call x1, Pallas kernels, body(): pl.pallas_call(kernel, out_shape=[jax.ShapeDtypeStruct((32, 128), f32), j...  109 us

profile of v7, /device:TPU:0, one launch (start us, length us, event | category | flops | bytes accessed | tf_op | source)
XLA Modules:
  0.0 111.6 jit_solution(5028679624497555383)
XLA Ops:
  0.6 109.0 %shard_map.68 = (f32[32,128]{1,0:T(8,128)}, f32[64,128]{1,0:T(8,128)}) custom-call(f32[2,8,8192]{2,1,0:T(8,128)} %bitcast.7, f32[2,16,4096]{2,1,0:T(8,128)} %bitcast.8, f32[32,128]{1,0:T(8,128)} %bitcast.11, f32[64,128]{1,0:T(8,128)} %bitcast.9, s32[16,64]{1,0:T(8,128)} %bitcast.13), custom_call_target="tpu_custom_call" | custom-call | tf_op jit(solution)/shard_map/pallas_call | solution.py:576
  109.6 0.0 copy-start
  109.7 1.3 %copy.9 = f32[4096]{0:T(1024)} copy(f32[4096]{0:T(1024)} %bitcast.12) | data formatting | bytes 32768
  111.0 0.0 copy-done
  111.0 0.6 copy.10
Async XLA Ops:
  109.6 1.3 %copy-start = (f32[64,128]{1,0:T(8,128)S(1)}, f32[64,128]{1,0:T(8,128)}, u32[]{:S(2)}) copy-start(f32[64,128]{1,0:T(8,128)} %get-tuple-element.5) | copy-start | bytes 98308
